TPU v7x, 512 devices: a whole 4x8x8 slice. The times are simulated.
512 devices in a mesh: wide: 32 (over y, x), narrow: 16 (over z, core).
Axes of the slice: x: 4, y: 8, z: 8, core: 2. Of those that a mesh axis runs over, the one named last changes fastest.
Arguments:
- feat_queries: bfloat16 [131072, 256], P(('wide', 'narrow')), may hold values from -6 to 6
- feat_keys: bfloat16 [131072, 256], P(('wide', 'narrow')), may hold values from -6 to 6
- values: bfloat16 [131072, 1024], P(('wide', 'narrow')), may hold values from -8 to 8
- window_queries: bfloat16 [131072, 1024], P(('wide', 'narrow')), may hold values from -150 to 150
- window_keys: bfloat16 [131072, 1024], P(('wide', 'narrow')), may hold values from -5 to 5
Outputs:
- mixed: bfloat16 [131072, 1024], P(('wide', 'narrow'))
All inputs are finite; a program needn't handle non-finite values.
Results may differ from a plain program's by a relative error of at most 0.0004.
The roundings to bfloat16 on the way count: a program that leaves them out, or rounds other values in their place, can miss the bound.
Values may be sent and summed in bfloat16 or wider, within the bound.
No kernel may reach another device: no remote copies, remote signals or barrier semaphores. Data moves between devices by JAX's collectives and lax.ppermute only.
A program may use at most 64 MiB of HBM per device.

v0:
```python
import jax
import jax.numpy as jnp
import numpy as np
from jax import lax
from jax.sharding import Mesh
from jax.sharding import PartitionSpec as P

HEADS = 16
WINDOW = 256
WIDE_NARROW = ("wide_0", "wide_1", "narrow_0", "narrow_1")
NARROW = ("narrow_0", "narrow_1")
WIDE = ("wide_0", "wide_1")


def neutral_like(array, identity):
    return jnp.zeros_like(array) + jnp.asarray(identity, array.dtype)


def entering(array, axes, combine, identity):
    before = start = neutral_like(array, identity)
    subtotal = array
    for axis in reversed(axes):
        devices, place = (lax.axis_size(axis), lax.axis_index(axis))
        pieces = lax.all_gather(subtotal, axis)
        inside, subtotal = (start, start)
        for k in range(devices):
            passed = k < place
            subtotal = combine(subtotal, pieces[k])
            inside = jnp.where(passed, subtotal, inside)
        before = combine(inside, before)
    return before


def sent_to_all(array, axis):
    copies = jnp.broadcast_to(array, (lax.axis_size(axis), *array.shape))
    return lax.all_to_all(copies, axis, split_axis=0, concat_axis=0, tiled=True)


def joined_along(parts, dim):
    parts = jnp.moveaxis(parts, 0, dim)
    shape = parts.shape
    return parts.reshape(*shape[:dim], shape[dim] * shape[dim + 1], *shape[dim + 2 :])


def collect(array, axis, dim):
    parts = sent_to_all(array, axis)
    return joined_along(parts, dim)


def from_behind(array, axis, by):
    devices = lax.axis_size(axis)
    pairs = [(i, i + by) for i in range(devices) if 0 <= i + by < devices]
    return lax.ppermute(array, axis, pairs)


def expand(x, heads):
    rows = x.shape[0]
    x = x.astype(jnp.float32).reshape(rows, heads, -1)
    width = x.shape[-1]
    first, second = np.triu_indices(width)
    weight = np.where(first == second, 1.0 / np.sqrt(2.0 * width), 1.0 / np.sqrt(1.0 * width))
    quad = x[..., first] * x[..., second] * jnp.asarray(weight, jnp.float32)
    ones = jnp.ones((rows, heads, 1), jnp.float32)
    return jnp.concatenate([ones, x / width**0.25, quad], -1).astype(jnp.bfloat16)


def add_pair(earlier, later):
    return earlier + later


def body(feat_queries, feat_keys, values, window_queries, window_keys):
    rows = values.shape[0]
    qf = expand(feat_queries, HEADS)
    kf = expand(feat_keys, HEADS)
    feats = qf.shape[-1]
    val3 = values.reshape(rows, HEADS, -1)
    own_state = jnp.einsum("shf,shv->fhv", kf, val3, preferred_element_type=jnp.float32).reshape(
        feats, -1
    )
    own_norm = jnp.sum(kf.astype(jnp.float32), 0).T
    prior_norm = entering(own_norm, WIDE_NARROW, add_pair, jnp.zeros_like(own_norm))
    pieces = lax.all_to_all(own_state[None], NARROW, split_axis=2, concat_axis=0, tiled=True)
    group_total = jnp.sum(pieces, 0, keepdims=True)
    inner = jnp.cumsum(pieces, 0) - pieces
    totals = collect(group_total, WIDE, 0)
    earlier = (
        lax.broadcasted_iota(jnp.int32, (totals.shape[0], 1, 1), 0) < lax.axis_index(WIDE)
    ).astype(jnp.float32)
    outer = jnp.sum(totals * earlier, 0, keepdims=True)
    prior_state = lax.all_to_all(inner + outer, NARROW, split_axis=0, concat_axis=2, tiled=True)[0]
    rim_keys, rim_values = from_behind((window_keys, values), WIDE_NARROW, 1)
    start = lax.axis_index(WIDE_NARROW) * rows
    scores = jnp.einsum("thf,shf->hts", qf, kf, preferred_element_type=jnp.float32)
    causal = lax.broadcasted_iota(jnp.int32, (rows, rows), 0) >= lax.broadcasted_iota(
        jnp.int32, (rows, rows), 1
    )
    scores = jnp.where(causal[None], scores, jnp.float32(0.0))
    intra_den = jnp.sum(scores, -1)
    intra_num = jnp.einsum(
        "hts,shv->thv", scores.astype(jnp.bfloat16), val3, preferred_element_type=jnp.float32
    )
    qwide = qf.astype(jnp.float32)
    cross_num = jnp.einsum(
        "thf,fhv->thv",
        qwide,
        prior_state.reshape(feats, HEADS, -1),
        precision=lax.Precision.HIGHEST,
    )
    cross_den = jnp.einsum("thf,fh->th", qwide, prior_norm, precision=lax.Precision.HIGHEST)
    linear = (intra_num + cross_num) / (intra_den.T + cross_den)[..., None]
    span = WINDOW
    keys3 = jnp.concatenate([rim_keys, window_keys], 0).reshape(span + rows, HEADS, -1)
    vals3 = jnp.concatenate([rim_values, values], 0).reshape(span + rows, HEADS, -1)
    query3 = window_queries.reshape(rows, HEADS, -1)
    logits = jnp.einsum(
        "thd,shd->hts", query3, keys3, preferred_element_type=jnp.float32
    ) / jnp.sqrt(jnp.float32(query3.shape[-1]))
    row = lax.broadcasted_iota(jnp.int32, (rows, span + rows), 0)
    col = lax.broadcasted_iota(jnp.int32, (rows, span + rows), 1)
    valid = (col > row) & (col <= row + span) & (col - span + start >= 0)
    logits = jnp.where(valid[None], logits, jnp.float32(-1e30))
    peak = jnp.max(logits, -1, keepdims=True)
    expo = jnp.where(valid[None], jnp.exp(logits - peak), jnp.float32(0.0))
    probs = (expo / jnp.sum(expo, -1, keepdims=True)).astype(jnp.bfloat16)
    window = jnp.einsum("hts,shv->thv", probs, vals3, preferred_element_type=jnp.float32)
    return (linear + window).reshape(rows, -1).astype(jnp.bfloat16)


def solution(mesh):
    finer = Mesh(mesh.devices.reshape(8, 4, 8, 2), ("wide_0", "wide_1", "narrow_0", "narrow_1"))
    placed = (
        P(WIDE_NARROW, None),
        P(WIDE_NARROW, None),
        P(WIDE_NARROW, None),
        P(WIDE_NARROW, None),
        P(WIDE_NARROW, None),
    )
    return jax.shard_map(
        body, mesh=finer, in_specs=placed, out_specs=P(WIDE_NARROW, None), check_vma=False
    )
```

profile of v0, /device:TPU:1, one launch (start us, length us, event | category | flops | bytes accessed | tf_op | source)
XLA Modules:
  0.0 201.8 jit_solution(6474089945362861485)
XLA Ops:
  0.0 1.0 copy.61
  1.0 0.2 copy.62
  1.2 0.7 pad_clamp_fusion.1
  1.9 0.7 pad_clamp_fusion
  2.5 0.8 gather_fusion
  3.4 0.0 copy-start.8
  3.4 2.2 %gather_fusion.1 = f32[136,256,16]{1,2,0:T(8,128)} fusion(f32[256,16,16]{0,1,2:T(8,128)S(1)} %copy.62, s32[1024]{0:T(1024)S(1)} %pad_clamp_fusion), kind=kCustom, calls=%fused_computation.1 | custom fusion | bytes 4456992 | tf_op jit(solution)/shard_map/gather | solution.py:62
  5.6 0.0 copy-done.8
  5.6 0.1 copy.66
  5.7 0.2 copy.67
  5.8 2.2 %gather_fusion.2 = f32[136,256,16]{1,2,0:T(8,128)} fusion(f32[256,16,16]{0,1,2:T(8,128)S(1)} %copy.67, s32[1024]{0:T(1024)S(1)} %pad_clamp_fusion.1), kind=kCustom, calls=%fused_computation.2 | custom fusion | bytes 4456992 | tf_op jit(solution)/shard_map/gather | solution.py:62
  8.1 2.1 %gather_fusion.3 = f32[136,256,16]{1,2,0:T(8,128)} fusion(f32[256,16,16]{0,1,2:T(8,128)S(1)} %copy.67, s32[1024]{0:T(1024)S(1)} %pad_clamp_fusion), kind=kCustom, calls=%fused_computation.3 | custom fusion | bytes 4456992 | tf_op jit(solution)/shard_map/gather | solution.py:62
  10.2 1.2 copy.71
  11.5 0.0 copy-start.6
  11.5 0.0 copy-done.14
  11.5 0.0 copy-start.11
  11.5 8.9 %fusion.20 = (bf16[256,16,136]{0,2,1:T(8,128)(2,1)}, bf16[256,16,136]{0,2,1:T(8,128)(2,1)S(1)}) fusion(f32[136,256,16]{1,2,0:T(8,128)} %gather_fusion.1, f32[136,256,16]{1,2,0:T(8,128)S(1)} %gather_fusion, f32[136]{0:T(256)S(1)} %copy-done.14, f32[136,256,16]{1,2,0:T(8,128)} %gather_fusion.3, f32[136,256,16]{1,2,0:T(8,128)} %gather_fusion.2), kind=kLoop, calls=%fused_computation.36 | loop fusion | flops 3342336 | bytes 11141664 | tf_op jit(solution)/shard_map/convert.7
  20.4 0.0 copy-done.6
  20.4 0.0 copy-done.11
  20.4 1.0 copy-done
  21.4 0.7 fusion.45
  22.1 2.0 %copy.73 = f32[1,153,1024]{1,0,2:T(1,128)} copy(f32[1,153,1024]{1,2,0:T(8,128)S(1)} %bitcast.85) | data formatting | bytes 1253376 | tf_op jit(solution)/shard_map/broadcast_in_dim;reshape | solution.py:82
  24.2 11.8 %all-to-all-start = ((f32[1,153,1024]{1,0,2:T(1,128)}), f32[1,153,1024]{1,0,2:T(1,128)S(1)}, u32[]{:S(2)}, u32[]{:S(2)}) async-start(f32[1,153,1024]{1,0,2:T(1,128)} %copy.73), calls=%async_computation | async-start | bytes 2097152 | tf_op jit(solution)/shard_map/all_to_all | solution.py:82
  36.0 3.5 %collective-permute-start = (bf16[256,1024]{1,0:T(8,128)(2,1)}, bf16[256,1024]{1,0:T(8,128)(2,1)}, u32[]{:S(2)}, u32[]{:S(2)}) collective-permute-start(bf16[256,1024]{1,0:T(8,128)(2,1)} %param.17), channel_id=1, source_target_pairs={{0,1},{1,2},{2,3},{3,4},{4,5},{5,6},{6,7},{7,8},{8,9},{9,10},{10,1... | collective-permute-start | bytes 1572872 | tf_op jit(solution)/shard_map/ppermute | solution.py:53
  39.5 2.1 %collective-permute-start.1 = (bf16[256,1024]{1,0:T(8,128)(2,1)}, bf16[256,1024]{1,0:T(8,128)(2,1)}, u32[]{:S(2)}, u32[]{:S(2)}) collective-permute-start(bf16[256,1024]{1,0:T(8,128)(2,1)} %param.19), channel_id=1, source_target_pairs={{0,1},{1,2},{2,3},{3,4},{4,5},{5,6},{6,7},{7,8},{8,9},{9,10},{10,1... | collective-permute-start | bytes 1572872 | tf_op jit(solution)/shard_map/ppermute | solution.py:53
  41.6 22.3 %all-to-all-done = f32[1,153,1024]{1,0,2:T(1,128)S(1)} async-done(((f32[1,153,1024]{1,0,2:T(1,128)}), f32[1,153,1024]{1,0,2:T(1,128)S(1)}, u32[]{:S(2)}, u32[]{:S(2)}) %all-to-all-start) | async-done | bytes 626720 | tf_op jit(solution)/shard_map/all_to_all | solution.py:82
  63.9 0.1 copy.86
  64.0 0.1 reduce_sum.45
  64.1 1.6 broadcast_in_dim.64
  65.7 18.9 %all-to-all-start.1 = ((f32[32,1,153,64]{2,3,1,0:T(8,128)}), f32[32,1,153,64]{2,3,1,0:T(8,128)S(1)}, u32[]{:S(2)}, u32[]{:S(2)}) async-start(f32[32,1,153,64]{2,3,1,0:T(8,128)} %broadcast_in_dim.64), calls=%async_computation.1 | async-start | bytes 4194304 | tf_op jit(solution)/shard_map/all_to_all | solution.py:36
  84.6 2.0 convert_reduce_fusion
  86.6 2.1 %copy.78 = bf16[256,1024]{0,1:T(8,128)(2,1)} copy(bf16[256,1024]{1,0:T(8,128)(2,1)} %param.18) | data formatting | bytes 1048576 | tf_op args[3]
  88.6 2.7 %all-gather.2 = f32[2,153,16]{1,2,0:T(8,128)S(1)} all-gather(f32[1,153,16]{1,2,0:T(8,128)S(1)} %bitcast.90), channel_id=2, replica_groups=mesh['wide_0'=8,'wide_1'=4,'narrow_0'=8,'narrow_1'=2] {'narrow_1'}, dimensions={0}, use_global_device_ids=true | all-gather | bytes 29376 | tf_op jit(solution)/shard_map/all_gather | solution.py:24
  91.3 20.3 %all-gather.3 = f32[8,153,16]{1,2,0:T(8,128)S(1)} all-gather(f32[1,153,16]{1,2,0:T(8,128)S(1)} %slice_add_fusion.17), channel_id=3, replica_groups=mesh['wide_0'=8,'wide_1'=4,'narrow_0'=8,'narrow_1'=2] {'narrow_0'}, dimensions={0}, use_global_device_ids=true | all-gather | bytes 88128 | tf_op jit(solution)/shard_map/all_gather | solution.py:24
  111.6 12.6 %all_gather.21 = f32[4,153,16]{1,2,0:T(8,128)S(1)} all-gather(f32[1,153,16]{1,2,0:T(8,128)S(1)} %get-tuple-element.5), channel_id=1, replica_groups=mesh['wide_0'=8,'wide_1'=4,'narrow_0'=8,'narrow_1'=2] {'wide_1'}, dimensions={0}, use_global_device_ids=true | all-gather | bytes 48960 | tf_op jit(solution)/shard_map/all_gather | solution.py:24
  124.2 20.9 %all_gather.22 = f32[8,153,16]{1,2,0:T(8,128)S(1)} all-gather(f32[1,153,16]{1,2,0:T(8,128)S(1)} %slice_add_fusion.7), channel_id=1, replica_groups=mesh['wide_0'=8,'wide_1'=4,'narrow_0'=8,'narrow_1'=2] {'wide_0'}, dimensions={0}, use_global_device_ids=true | all-gather | bytes 88128 | tf_op jit(solution)/shard_map/all_gather | solution.py:24
  145.1 0.0 copy-start.9
  145.2 0.0 copy-start.4
  145.2 2.2 %fusion.32 = f32[16,1,256]{2,1,0:T(1,128)S(1)} fusion(f32[153,16,1]{0,1,2:T(8,128)S(1)} %fusion.30, bf16[256,16,136]{0,2,1:T(8,128)(2,1)} %get-tuple-element.7, bf16[256,16,16]{0,2,1:T(8,128)(2,1)S(1)} %multiply_convert_fusion.1, bf16[153]{0:T(256)(128)(2,1)} %copy-done.11), kind=kOutput, calls=%fused_computation.74 | convolution fusion | flops 11280384 | bytes 1271666 | tf_op jit(solution)/shard_map/thf,fh->th/dot_general | solution.py:109
  147.4 0.0 copy-done.1
  147.4 0.0 copy-done.2
  147.4 0.0 copy-done.12
  147.4 3.0 %select_reduce_fusion = (f32[16,256]{1,0:T(8,128)S(1)}, bf16[16,256,256]{1,2,0:T(8,128)(2,1)}) fusion(pred[256,256]{0,1:T(8,128)(4,1)S(1)} %iota_compare_fusion.2, bf16[256,16,136]{0,2,1:T(8,128)(2,1)S(1)} %copy-done.1, bf16[256,16,16]{0,2,1:T(8,128)(2,1)S(1)} %multiply_convert_fusion, bf16[153]{0:T(256)(128)(2,1)S(1)} %copy-done.12, ...), kind=kOutput, calls=%fused_computation.13 | convolution fusion | flops 331526144 | bytes 4669746 | tf_op jit(solution)/shard_map/thf,shf->hts/dot_general | solution.py:93
  150.4 0.0 copy-done.9
  150.4 0.0 all-to-all-done.1
  150.4 0.2 fusion.11
  150.7 1.1 fusion.22
  151.8 14.6 %all-to-all-start.2 = ((f32[16,153,64]{1,2,0:T(8,128)}), f32[16,153,64]{1,2,0:T(8,128)S(1)}, u32[]{:S(2)}, u32[]{:S(2)}) async-start(f32[16,153,64]{1,2,0:T(8,128)} %fusion.22), calls=%async_computation.2 | async-start | bytes 2097152 | tf_op jit(solution)/shard_map/all_to_all | solution.py:90
  166.3 0.2 fusion.27
  166.5 0.0 collective-permute-done.1
  166.5 1.3 pad_maximum_fusion.3
  167.8 1.4 copy.77
  169.1 0.0 collective-permute-done
  169.2 1.3 pad_maximum_fusion.2
  170.4 0.5 copy.76
  171.0 8.0 %fusion.46 = (f32[16,256]{1,0:T(8,128)S(1)}, f32[16,256,512]{1,2,0:T(8,128)}) fusion(pred[256,512]{0,1:T(8,128)(4,1)S(1)} %fusion.27, bf16[512,16,64]{0,2,1:T(8,128)(2,1)} %bitcast.84, bf16[256,16,64]{0,2,1:T(8,128)(2,1)} %bitcast.88), kind=kOutput, calls=%fused_computation.94 | convolution fusion | flops 278921728 | bytes 10108928 | tf_op jit(solution)/shard_map/sub | solution.py:123
  179.0 15.3 %all-to-all-done.2 = f32[16,153,64]{1,2,0:T(8,128)S(1)} async-done(((f32[16,153,64]{1,2,0:T(8,128)}), f32[16,153,64]{1,2,0:T(8,128)S(1)}, u32[]{:S(2)}, u32[]{:S(2)}) %all-to-all-start.2) | async-done | bytes 626720 | tf_op jit(solution)/shard_map/all_to_all | solution.py:90
  194.3 0.0 copy-done.3
  194.3 0.0 copy-start.7
  194.3 1.1 convolution_bitcast_fusion
  195.5 0.6 copy-done.15
  196.1 0.5 fusion.19
  196.6 4.3 %fusion.18 = bf16[256,16,64]{0,2,1:T(8,128)(2,1)S(1)} fusion(f32[256,16,64]{0,2,1:T(8,128)S(1)} %fusion.19, bf16[512,16,64]{0,2,1:T(8,128)(2,1)S(1)} %bitcast.83, f32[16,256,512]{1,2,0:T(8,128)} %get-tuple-element.12, f32[16,256]{1,0:T(8,128)S(1)} %get-tuple-element.11), kind=kOutput, calls=%fused_computation.34 | convolution fusion | flops 273154048 | bytes 11026432 | tf_op jit(solution)/shard_map/hts,shv->thv/dot_general | solution.py:125
  200.8 1.0 copy.80
  (27 shorter events, 0.2 us)
Async XLA Ops:
  3.4 2.2 %copy-start.8 = (bf16[256,256]{1,0:T(8,128)(2,1)S(1)}, bf16[256,256]{1,0:T(8,128)(2,1)}, u32[]{:S(2)}) copy-start(bf16[256,256]{1,0:T(8,128)(2,1)} %param.16) | copy-start | bytes 393220
  8.1 3.5 %copy-start.14 = (f32[136]{0:T(256)S(1)}, f32[136]{0:T(256)}, u32[]{:S(2)}) copy-start(f32[136]{0:T(256)} %constant.76.clone) | copy-start | bytes 1636
  11.5 8.9 %copy-start.6 = (bf16[256,1024]{0,1:T(8,128)(2,1)}, bf16[256,1024]{0,1:T(8,128)(2,1)S(1)}, u32[]{:S(2)}) copy-start(bf16[256,1024]{0,1:T(8,128)(2,1)S(1)} %copy.71) | copy-start | bytes 1572868
  11.5 8.9 %copy-start.11 = (bf16[153]{0:T(256)(128)(2,1)}, bf16[153]{0:T(256)(128)(2,1)S(1)}, u32[]{:S(2)}) copy-start(bf16[153]{0:T(256)(128)(2,1)S(1)} %pad.7.clone) | copy-start | bytes 922
  20.4 1.0 copy-start
  24.2 39.8 %all-to-all-start = ((f32[1,153,1024]{1,0,2:T(1,128)}), f32[1,153,1024]{1,0,2:T(1,128)S(1)}, u32[]{:S(2)}, u32[]{:S(2)}) async-start(f32[1,153,1024]{1,0,2:T(1,128)} %copy.73), calls=%async_computation | async-start | bytes 2097152 | tf_op jit(solution)/shard_map/all_to_all | solution.py:82
  36.0 133.2 %collective-permute-start = (bf16[256,1024]{1,0:T(8,128)(2,1)}, bf16[256,1024]{1,0:T(8,128)(2,1)}, u32[]{:S(2)}, u32[]{:S(2)}) collective-permute-start(bf16[256,1024]{1,0:T(8,128)(2,1)} %param.17), channel_id=1, source_target_pairs={{0,1},{1,2},{2,3},{3,4},{4,5},{5,6},{6,7},{7,8},{8,9},{9,10},{10,1... | collective-permute-start | bytes 1572872 | tf_op jit(solution)/shard_map/ppermute | solution.py:53
  39.5 127.0 %collective-permute-start.1 = (bf16[256,1024]{1,0:T(8,128)(2,1)}, bf16[256,1024]{1,0:T(8,128)(2,1)}, u32[]{:S(2)}, u32[]{:S(2)}) collective-permute-start(bf16[256,1024]{1,0:T(8,128)(2,1)} %param.19), channel_id=1, source_target_pairs={{0,1},{1,2},{2,3},{3,4},{4,5},{5,6},{6,7},{7,8},{8,9},{9,10},{10,1... | collective-permute-start | bytes 1572872 | tf_op jit(solution)/shard_map/ppermute | solution.py:53
  65.7 84.7 %all-to-all-start.1 = ((f32[32,1,153,64]{2,3,1,0:T(8,128)}), f32[32,1,153,64]{2,3,1,0:T(8,128)S(1)}, u32[]{:S(2)}, u32[]{:S(2)}) async-start(f32[32,1,153,64]{2,3,1,0:T(8,128)} %broadcast_in_dim.64), calls=%async_computation.1 | async-start | bytes 4194304 | tf_op jit(solution)/shard_map/all_to_all | solution.py:36
  88.6 58.8 %copy-start.1 = (bf16[256,16,136]{0,2,1:T(8,128)(2,1)S(1)}, bf16[256,16,136]{0,2,1:T(8,128)(2,1)}, u32[]{:S(2)}) copy-start(bf16[256,16,136]{0,2,1:T(8,128)(2,1)} %copy-done) | copy-start | bytes 3342340
  88.6 58.8 %copy-start.2 = (bf16[256,16,136]{0,2,1:T(8,128)(2,1)S(1)}, bf16[256,16,136]{0,2,1:T(8,128)(2,1)}, u32[]{:S(2)}) copy-start(bf16[256,16,136]{0,2,1:T(8,128)(2,1)} %get-tuple-element.7) | copy-start | bytes 3342340
  88.6 58.8 %copy-start.12 = (bf16[153]{0:T(256)(128)(2,1)S(1)}, bf16[153]{0:T(256)(128)(2,1)}, u32[]{:S(2)}) copy-start(bf16[153]{0:T(256)(128)(2,1)} %copy-done.11) | copy-start | bytes 922
  145.1 5.3 %copy-start.9 = (pred[256,256]{0,1:T(8,128)(4,1)}, pred[256,256]{0,1:T(8,128)(4,1)S(1)}, u32[]{:S(2)}) copy-start(pred[256,256]{0,1:T(8,128)(4,1)S(1)} %iota_compare_fusion.2) | copy-start | bytes 196612
  145.2 5.2 %copy-start.4 = (bf16[256,16,16]{0,2,1:T(8,128)(2,1)}, bf16[256,16,16]{0,2,1:T(8,128)(2,1)S(1)}, u32[]{:S(2)}) copy-start(bf16[256,16,16]{0,2,1:T(8,128)(2,1)S(1)} %multiply_convert_fusion.1) | copy-start | bytes 393220
  151.8 42.5 %all-to-all-start.2 = ((f32[16,153,64]{1,2,0:T(8,128)}), f32[16,153,64]{1,2,0:T(8,128)S(1)}, u32[]{:S(2)}, u32[]{:S(2)}) async-start(f32[16,153,64]{1,2,0:T(8,128)} %fusion.22), calls=%async_computation.2 | async-start | bytes 2097152 | tf_op jit(solution)/shard_map/all_to_all | solution.py:90
  171.0 23.3 %copy-start.3 = (bf16[256,16,136]{0,2,1:T(8,128)(2,1)S(1)}, bf16[256,16,136]{0,2,1:T(8,128)(2,1)}, u32[]{:S(2)}) copy-start(bf16[256,16,136]{0,2,1:T(8,128)(2,1)} %get-tuple-element.7) | copy-start | bytes 3342340
  171.0 23.3 %copy-start.5 = (bf16[256,16,16]{0,2,1:T(8,128)(2,1)S(1)}, bf16[256,16,16]{0,2,1:T(8,128)(2,1)}, u32[]{:S(2)}) copy-start(bf16[256,16,16]{0,2,1:T(8,128)(2,1)} %copy-done.4) | copy-start | bytes 393220
  171.0 23.3 %copy-start.13 = (bf16[153]{0:T(256)(128)(2,1)S(1)}, bf16[153]{0:T(256)(128)(2,1)}, u32[]{:S(2)}) copy-start(bf16[153]{0:T(256)(128)(2,1)} %copy-done.11) | copy-start | bytes 922
  179.0 16.4 %copy-start.10 = (pred[256,256]{0,1:T(8,128)(4,1)S(1)}, pred[256,256]{0,1:T(8,128)(4,1)}, u32[]{:S(2)}) copy-start(pred[256,256]{0,1:T(8,128)(4,1)} %copy-done.9) | copy-start | bytes 196612
  194.3 1.1 copy-start.7
  194.3 1.8 copy-start.15
where the time goes:
time: 203 us; the launch traced here: 202 us
  blocking collectives  56.4 us (28%)
  starting transfers between devices  50.9 us (25%)
  waiting for transfers between devices  37.6 us (19%)
  local copies, waits for them, and re-layouts  20.4 us (10%)
  matrix products  19.7 us (10%)
  other arithmetic  16.5 us (8%)
    all_gather x4, blocking collectives, entering(): pieces = lax.all_gather(subtotal, axis)  56.4 us
    all_to_all x1, waiting for transfers between devices, body(): lax.all_to_all(own_state[None], NARROW, split_axis=2, concat_axis=0, tile...  22.3 us
    all_to_all x1, starting transfers between devices, sent_to_all(): return lax.all_to_all(copies, axis, split_axis=0, concat_axis=0, tiled=True)  18.9 us
    all_to_all x1, waiting for transfers between devices, body(): lax.all_to_all(inner + outer, NARROW, split_axis=0, concat_axis=2, tiled=...  15.3 us
    all_to_all x1, starting transfers between devices, body(): lax.all_to_all(inner + outer, NARROW, split_axis=0, concat_axis=2, tiled=...  14.6 us
    all_to_all x1, starting transfers between devices, body(): lax.all_to_all(own_state[None], NARROW, split_axis=2, concat_axis=0, tile...  11.8 us
    another operation x3, other arithmetic  8.92 us
    sub x1, matrix products, body(): expo = jnp.where(valid[None], jnp.exp(logits - peak), jnp.float32(0.0))  8.02 us
  transfers between devices with their start and end apart: 5, of which 2 were waited for; matrix products, arithmetic and copies ran while one was open for 12% of the time, Pallas kernels for 0%

commit v1 on v0

v1 whole, which is shorter than its diff:
```python
import jax
import jax.numpy as jnp
import numpy as np
from jax import lax
from jax.experimental import pallas as pl
from jax.experimental.pallas import tpu as pltpu
from jax.sharding import Mesh
from jax.sharding import PartitionSpec as P

HEADS = 16
PAIRS = HEADS // 2
DIM = 16
ROWS = 256
FEATS = 153
FROWS = 160
PIECES = 32
PAIR_ROWS = 160
PROWS = 20
PIECE = (PROWS // 4, 4, 128)
TAIL = slice(152, 160)
VALUES = HEADS * 64
LANES = 128
AXES = ("y", "x", "z", "c")
F32 = jnp.float32
BF16 = jnp.bfloat16
W_DIAG = np.float32(1.0 / np.sqrt(2.0 * DIM))
W_OFF = np.float32(1.0 / np.sqrt(1.0 * DIM))
SCALE = np.float32(1.0 / DIM**0.25)
NT = (((1,), (1,)), ((), ()))


def features(x):
    twice = jnp.concatenate([x, x], 0)
    quarter = twice * W_OFF
    parts = [x * SCALE, x * x * W_DIAG]
    for shift in range(1, 8):
        parts.append(x * quarter[shift : shift + DIM])
    parts.append(x[:8] * quarter[8:16])
    one = lax.broadcasted_iota(jnp.int32, (8, x.shape[1]), 0) == 0
    parts.append(jnp.where(one, F32(1.0), F32(0.0)))
    return jnp.concatenate(parts, 0)


def low_lanes(rows):
    return lax.broadcasted_iota(jnp.int32, (rows, LANES), 1) < 64


def state_kernel(core_ref, fk_hbm, v_hbm, out_ref, fk_ref, v_ref, kt_ref, sems):
    half = VALUES // 2
    copies = [pltpu.make_async_copy(fk_hbm, fk_ref, sems.at[0])]
    for i in range(2):
        lanes = pl.ds(i * half, half)
        copies.append(pltpu.make_async_copy(v_hbm.at[:, lanes], v_ref.at[:, lanes], sems.at[1 + i]))
    for copy in copies:
        copy.start()
    first = core_ref[0] * (PAIRS // 2)
    copies[0].wait()
    kt_ref[...] = fk_ref[...].astype(F32).T
    lane = lax.broadcasted_iota(jnp.int32, (FROWS, LANES), 1)
    low = lane < 64
    vlow = low_lanes(ROWS)
    zcols = jnp.zeros((FROWS, LANES), F32)
    copies[1].wait()
    copies[2].wait()
    for i in range(PAIRS):
        pair = lax.rem(first + i, PAIRS)
        x = kt_ref[pl.ds(pl.multiple_of(pair * 32, 32), 32), :]
        v = v_ref[:, pl.ds(pl.multiple_of(pair * LANES, LANES), LANES)]
        one = jnp.ones_like(v)
        fa = features(x[:DIM]).astype(BF16)
        fb = features(x[DIM:]).astype(BF16)
        sa = jnp.dot(fa, jnp.where(vlow, v, one), preferred_element_type=F32)
        sb = jnp.dot(fb, jnp.where(vlow, one, v), preferred_element_type=F32)
        out_ref[i, :FROWS] = jnp.where(low, sa, sb)
        z = jnp.where(low, sb, sa)
        zcols = jnp.where((lane == i) | (lane == 64 + i), z, zcols)
    zrows = zcols.T
    blank = jnp.zeros((8, 2 * LANES - FROWS), F32)
    row = lax.broadcasted_iota(jnp.int32, (8, LANES), 0)
    for i in range(PAIRS):
        tail = out_ref[i, TAIL]
        for at, src in ((1, 64 + i), (3, i)):
            z = jnp.concatenate([jnp.broadcast_to(zrows[src : src + 1], (8, FROWS)), blank], 1)
            tail = jnp.where(row == at, z[:, :LANES], tail)
            tail = jnp.where(row == at + 1, z[:, LANES:], tail)
        out_ref[i, TAIL] = tail


def inner_kernel(p_ref, out_ref):
    run = jnp.zeros((PROWS, LANES), F32)
    for k in range(PIECES):
        at = slice(PROWS * k, PROWS * (k + 1))
        out_ref[at] = run
        run = run + p_ref[at]


def spread_kernel(y_ref, inner_ref, py_ref, out_ref):
    y = y_ref[0]
    outer = jnp.zeros((PROWS, LANES), F32)
    for k in range(8):
        outer = outer + jnp.where(k < y, py_ref[PROWS * k : PROWS * (k + 1)], F32(0.0))
    twice = jnp.concatenate([outer, outer], 0)
    for k in range(PIECES // 2):
        at = slice(2 * PROWS * k, 2 * PROWS * (k + 1))
        out_ref[at] = inner_ref[at] + twice


def split3(x):
    hi = x.astype(BF16)
    rest = x - hi.astype(F32)
    mid = rest.astype(BF16)
    lo = (rest - mid.astype(F32)).astype(BF16)
    return hi, mid, lo


def norm_columns(tails):
    rows = []
    for tail in tails:
        for row in (1, 3):
            rows.append(jnp.concatenate([tail[row : row + 1], tail[row + 1 : row + 2]], 1))
    rows.append(jnp.zeros((LANES - HEADS, 2 * LANES), F32))
    return jnp.concatenate(rows, 0).T[:FROWS]


def cross(qfs, s, zcols, at):
    low, tlow = low_lanes(FROWS), low_lanes(ROWS)
    s = jnp.where(lax.broadcasted_iota(jnp.int32, s.shape, 0) < FEATS, s, F32(0.0))
    res = []
    for h in range(2):
        z = jnp.broadcast_to(zcols[:, at + h : at + h + 1], (FROWS, LANES))
        hi, mid, lo = split3(jnp.where(low, s, z) if h == 0 else jnp.where(low, z, s))
        big = jnp.dot(qfs[h], jnp.concatenate([hi, mid], 1), preferred_element_type=F32)
        res.append(big[:, :LANES] + (big[:, LANES:] + jnp.dot(qfs[h], lo, preferred_element_type=F32)))
    num = jnp.where(tlow, res[0], res[1])
    den = pltpu.roll(jnp.where(tlow, res[1], res[0]), 64, 1)
    return num, den


def intra_kernel(core_ref, fq_ref, fk_ref, v_ref, sib_ref, qf_hbm, num_hbm, den_hbm, qt_ref, kt_ref, qf_ref, num_ref, den_ref, sems):
    second = core_ref[0] == 1
    qt_ref[...] = fq_ref[...].astype(F32).T
    kt_ref[...] = fk_ref[...].astype(F32).T
    low = low_lanes(ROWS)
    causal = lax.broadcasted_iota(jnp.int32, (ROWS, ROWS), 0) >= lax.broadcasted_iota(
        jnp.int32, (ROWS, ROWS), 1
    )
    zcols = norm_columns([sib_ref[i, TAIL] for i in range(PAIRS)])
    zcols = jnp.where(second, zcols, F32(0.0))
    copies = []
    for quad in range(PAIRS // 2):
        dens, rounded, qfs = [], [], []
        for h in range(4 * quad, 4 * quad + 4):
            rows = slice(h * DIM, (h + 1) * DIM)
            qf = features(qt_ref[rows, :]).T.astype(BF16)
            kf = features(kt_ref[rows, :]).astype(BF16)
            qf_ref[h] = qf
            qfs.append(qf)
            a = jnp.dot(qf, kf, preferred_element_type=F32)
            a = jnp.where(causal, a, F32(0.0))
            dens.append(jnp.sum(a, -1, keepdims=True))
            rounded.append(a.astype(BF16))
        wide = slice(quad * 256, (quad + 1) * 256)
        nums = jnp.dot(jnp.concatenate(rounded, 0), v_ref[:, wide], preferred_element_type=F32)
        for p in range(2):
            pair = 2 * quad + p
            s = jnp.where(second, sib_ref[pair], F32(0.0))
            num, den = cross(qfs[2 * p : 2 * p + 2], s, zcols, 2 * pair)
            lanes = slice(pair * LANES, (pair + 1) * LANES)
            here = slice(p * LANES, (p + 1) * LANES)
            n0 = nums[2 * p * ROWS : (2 * p + 1) * ROWS, here]
            n1 = nums[(2 * p + 1) * ROWS : (2 * p + 2) * ROWS, here]
            num_ref[:, lanes] = num + jnp.where(low, n0, n1)
            den_ref[:, lanes] = den + jnp.where(low, dens[2 * p], dens[2 * p + 1])
        heads = pl.ds(4 * quad, 4)
        lanes = pl.ds(quad * 256, 256)
        for k, (src, dst) in enumerate(
            (
                (qf_ref.at[heads], qf_hbm.at[heads]),
                (num_ref.at[:, lanes], num_hbm.at[:, lanes]),
                (den_ref.at[:, lanes], den_hbm.at[:, lanes]),
            )
        ):
            copy = pltpu.make_async_copy(src, dst, sems.at[k, quad])
            copy.start()
            copies.append(copy)
    for copy in copies:
        copy.wait()


def window_kernel(start_ref, q_ref, k_ref, v_ref, hk_ref, hv_ref, out_hbm, out_ref, sems):
    half = ROWS // 2
    inside = start_ref[0] > 0
    r = lax.broadcasted_iota(jnp.int32, (4 * half, ROWS), 0) % half
    c = lax.broadcasted_iota(jnp.int32, (4 * half, ROWS), 1)
    masks = (
        ((c > r) & inside, (c <= r)[:, :half]),
        ((c > r)[:, :half] & inside, c <= r + half),
    )
    worst = F32(-1e30)
    head = lax.broadcasted_iota(jnp.int32, (half, 256), 1) // 64
    copies = []
    for quad in range(PAIRS // 2):
        lanes = slice(quad * 256, (quad + 1) * 256)
        for b in range(2):
            mine = slice(half * b, half * (b + 1))
            q = q_ref[mine, lanes] * BF16(0.125)
            hs = slice(half * b, ROWS)
            os = slice(0, half * (b + 1))
            qs = jnp.concatenate([jnp.where(head == h, q, jnp.zeros_like(q)) for h in range(4)], 0)
            lh = lax.dot_general(qs, hk_ref[hs, lanes], NT, preferred_element_type=F32)
            lo = lax.dot_general(qs, k_ref[os, lanes], NT, preferred_element_type=F32)
            lh = jnp.where(masks[b][0], lh, worst)
            lo = jnp.where(masks[b][1], lo, worst)
            peak = jnp.maximum(jnp.max(lh, -1, keepdims=True), jnp.max(lo, -1, keepdims=True))
            eh = jnp.exp(lh - peak)
            eo = jnp.exp(lo - peak)
            inv = F32(1.0) / (jnp.sum(eh, -1, keepdims=True) + jnp.sum(eo, -1, keepdims=True))
            ph = (eh * inv).astype(BF16)
            po = (eo * inv).astype(BF16)
            o = jnp.dot(ph, hv_ref[hs, lanes], preferred_element_type=F32) + jnp.dot(
                po, v_ref[os, lanes], preferred_element_type=F32
            )
            res = o[:half]
            for h in range(1, 4):
                res = jnp.where(head == h, o[h * half : (h + 1) * half], res)
            out_ref[mine, lanes] = res
        at = pl.ds(quad * 256, 256)
        copy = pltpu.make_async_copy(out_ref.at[:, at], out_hbm.at[:, at], sems.at[quad])
        copy.start()
        copies.append(copy)
    for copy in copies:
        copy.wait()


def final_kernel(core_ref, mine_ref, other_ref, qf_hbm, num_hbm, den_hbm, win_hbm, out_ref, qf_ref, num_ref, den_ref, win_ref, sems):
    first = core_ref[0] * (PAIRS // 2)
    half = PAIRS // 2
    copies = []
    for i in range(4):
        quad = lax.rem(core_ref[0] * 2 + i, 4)
        heads = pl.ds(4 * quad, 4)
        lanes = pl.ds(pl.multiple_of(quad * 256, 256), 256)
        group = []
        for k, (src, dst) in enumerate(
            (
                (qf_hbm.at[heads], qf_ref.at[heads]),
                (num_hbm.at[:, lanes], num_ref.at[:, lanes]),
                (den_hbm.at[:, lanes], den_ref.at[:, lanes]),
                (win_hbm.at[:, lanes], win_ref.at[:, lanes]),
            )
        ):
            copy = pltpu.make_async_copy(src, dst, sems.at[k, i])
            copy.start()
            group.append(copy)
        copies.append(group)
    refs = [mine_ref] * half + [other_ref] * half
    zcols = norm_columns([refs[i][i % half, TAIL] for i in range(PAIRS)])
    for i in range(PAIRS):
        if i % 2 == 0:
            for copy in copies[i // 2]:
                copy.wait()
        pair = lax.rem(first + i, PAIRS)
        lanes = pl.ds(pl.multiple_of(pair * LANES, LANES), LANES)
        qfs = [qf_ref[pair * 2], qf_ref[pair * 2 + 1]]
        num, den = cross(qfs, refs[i][i % half], zcols, 2 * i)
        linear = (num + num_ref[:, lanes]) / (den + den_ref[:, lanes])
        out_ref[:, lanes] = (linear + win_ref[:, lanes]).astype(BF16)


def spec(kind=pltpu.VMEM):
    return pl.BlockSpec(memory_space=kind)


def call(kernel, ins, outs, scratch, flops, moved, name):
    made = pl.pallas_call(
        kernel,
        out_shape=[pltpu.HBM(o.shape, o.dtype) if k == HB else o for o, k in outs],
        in_specs=[spec(k) for k in ins],
        out_specs=[spec(k) for _, k in outs],
        scratch_shapes=scratch,
        compiler_params=pltpu.CompilerParams(vmem_limit_bytes=40 * 2**20),
        cost_estimate=pl.CostEstimate(flops=flops, bytes_accessed=moved, transcendentals=0),
        name=name,
    )
    return lambda *arrays: made(
        *(pltpu.with_memory_space_constraint(a, k) if k == HB else a for a, k in zip(arrays, ins, strict=True))
    )


def shape(*dims, dtype=F32):
    return jax.ShapeDtypeStruct(dims, dtype)


SM, VM, HB = pltpu.SMEM, pltpu.VMEM, pltpu.HBM
TURNED = pltpu.VMEM((256, ROWS), F32)
WIDE = pltpu.VMEM((ROWS, VALUES), F32)
QF = (HEADS, ROWS, FROWS)


def own_state(core, fk, v):
    return call(
        state_kernel, [SM, HB, HB], [(shape(PAIRS, PAIR_ROWS, LANES), VM)],
        [pltpu.VMEM((ROWS, 256), BF16), pltpu.VMEM((ROWS, VALUES), BF16), TURNED, pltpu.SemaphoreType.DMA((3,))],
        10**9, 5 * 10**6, "state",
    )(core, fk, v)[0]


def inner(pieces):
    flat = shape(PIECES * PROWS, LANES)
    return call(inner_kernel, [VM], [(flat, VM)], [], 2 * 10**9, 10**6, "inner")(pieces.reshape(flat.shape))[0]


def spread(y, before, rows):
    return call(spread_kernel, [SM, VM, VM], [(shape(PIECES * PROWS, LANES), VM)], [], 10**6, 10**6, "spread")(
        y, before, rows.reshape(-1, LANES)
    )[0]


def intra(core, fq, fk, v, sib):
    wide = shape(ROWS, VALUES)
    return call(
        intra_kernel, [SM, VM, VM, VM, VM], [(shape(*QF, dtype=BF16), HB), (wide, HB), (wide, HB)],
        [TURNED, TURNED, pltpu.VMEM(QF, BF16), WIDE, WIDE, pltpu.SemaphoreType.DMA((3, 4))],
        2000000000, 16 * 10**6, "intra",
    )(core, fq, fk, v, sib)


def window(start, q, k, v, hk, hv):
    return call(
        window_kernel, [SM] + [VM] * 5, [(shape(ROWS, VALUES), HB)], [WIDE, pltpu.SemaphoreType.DMA((4,))],
        2 * 10**9, 16 * 10**6, "window",
    )(start, q, k, v, hk, hv)[0]


def final(core, mine, other, qf, num, den, win):
    return call(
        final_kernel, [SM, VM, VM] + [HB] * 4, [(shape(ROWS, VALUES, dtype=BF16), VM)],
        [pltpu.VMEM(QF, BF16), WIDE, WIDE, WIDE, pltpu.SemaphoreType.DMA((4, 4))], 2 * 10**9, 10**7, "final",
    )(core, mine, other, qf, num, den, win)[0]


def exchange(array, axes):
    return lax.all_to_all(array, axes, split_axis=0, concat_axis=0, tiled=True)


def swap(array):
    return lax.ppermute(array, "c", [(0, 1), (1, 0)])


def scalar(value):
    return jnp.asarray(value, jnp.int32).reshape(1)


def after(first, *arrays):
    return lax.optimization_barrier((first, *arrays))


def body(fq, fk, v, wq, wk):
    core = scalar(lax.axis_index("c"))
    start = scalar(lax.axis_index(AXES))
    state = own_state(core, fk, v)
    sib = swap(state)
    half = PAIRS // 2
    chip = (state[:half] + sib[half:]).reshape(PIECES, *PIECE)
    chip, fq, fk = after(chip, fq, fk)
    pieces = exchange(chip, ("x", "z"))
    qf, num, den = intra(core, fq, fk, v, sib)
    pieces, qf, num, den = after(pieces, qf, num, den)
    total = jnp.broadcast_to(jnp.sum(pieces, 0), (8, *PIECE))
    total, pieces, wk_out, v_out = after(total, pieces, wk, v)
    rows = exchange(total, "y")
    count = lax.axis_size(AXES)
    pairs = [(i, i + 1) for i in range(count - 1)]
    hk = lax.ppermute(wk_out, AXES, pairs)
    hv = lax.ppermute(v_out, AXES, pairs)
    before = inner(pieces)
    rows, before = after(rows, before)
    back = spread(scalar(lax.axis_index("y")), before, rows)
    back, wq = after(back.reshape(PIECES, *PIECE), wq)
    mine = exchange(back, ("x", "z"))
    win = window(start, wq, wk, v, hk, hv)
    mine, win = after(mine, win)
    mine = mine.reshape(half, PAIR_ROWS, LANES)
    other = swap(mine)
    return final(core, mine, other, qf, num, den, win)


def solution(mesh):
    finer = Mesh(mesh.devices.reshape(8, 4, 8, 2), AXES)
    placed = P(AXES, None)
    return jax.shard_map(
        body, mesh=finer, in_specs=(placed,) * 5, out_specs=placed, check_vma=False
    )
```

time: 203 us -> 79.8 us (0.39)
  the two profiles are of different devices: /device:TPU:1 before, /device:TPU:33 now
where the time goes in v1:
time: 79.8 us; the launch traced here: 79.3 us
  starting transfers between devices  41.9 us (53%)
  Pallas kernels  18 us (23%)
  waiting for transfers between devices  17.7 us (22%)
  other arithmetic  0.84 us (1%)
    all_to_all x3, starting transfers between devices, exchange(): return lax.all_to_all(array, axes, split_axis=0, concat_axis=0, tiled=True)  24.2 us
    pallas_call x6, Pallas kernels, call(): made(*(pltpu.with_memory_space_constraint(a, k) if k == HB else a for a,...  18 us
    ppermute x1, starting transfers between devices, body(): hk = lax.ppermute(wk_out, AXES, pairs)  7.93 us
    ppermute x2, starting transfers between devices, swap(): return lax.ppermute(array, 'c', [(0, 1), (1, 0)])  7.79 us
    ppermute x1, waiting for transfers between devices, body(): hv = lax.ppermute(v_out, AXES, pairs)  7.55 us
    all_to_all x3, waiting for transfers between devices, exchange(): return lax.all_to_all(array, axes, split_axis=0, concat_axis=0, tiled=True)  7.19 us
    ppermute x2, waiting for transfers between devices, swap(): return lax.ppermute(array, 'c', [(0, 1), (1, 0)])  2.94 us
    ppermute x1, starting transfers between devices, body(): hv = lax.ppermute(v_out, AXES, pairs)  1.92 us
  transfers between devices with their start and end apart: 7, of which 5 were waited for; matrix products, arithmetic and copies ran while one was open for 0% of the time, Pallas kernels for 15%

profile of v1, /device:TPU:33, one launch (start us, length us, event | category | flops | bytes accessed | tf_op | source)
XLA Modules:
  0.0 79.3 jit_solution(17022512983021700837)
XLA Ops:
  0.0 0.0 copy-start
  0.0 0.0 copy-start.3
  0.0 0.0 copy-start.4
  0.0 1.9 %state.1 = f32[8,160,128]{2,1,0:T(8,128)S(1)} custom-call(s32[1]{0:T(128)} %bitcast.core_ref, bf16[256,256]{1,0:T(8,128)(2,1)} %fk_ref, bf16[256,1024]{1,0:T(8,128)(2,1)} %v_ref.3), custom_call_target="tpu_custom_call" | custom-call | flops 1000000000 | bytes 5000000 | tf_op jit(solution)/shard_map/state/pallas_call | solution.py:285
  1.9 2.6 %collective-permute-start = (f32[8,160,128]{2,1,0:T(8,128)S(1)}, f32[8,160,128]{2,1,0:T(8,128)S(1)}, u32[]{:S(2)}, u32[]{:S(2)}) collective-permute-start(f32[8,160,128]{2,1,0:T(8,128)S(1)} %state.1), channel_id=1, source_target_pairs={{0,1},{1,0},{2,3},{3,2},{4,5},{5,4},{6,7},{7,6},{8,9},{9,8},{10,11... | collective-permute-start | bytes 1966088 | tf_op jit(solution)/shard_map/ppermute | solution.py:347
  4.5 1.7 %collective-permute-done.sib_ref = f32[8,160,128]{2,1,0:T(8,128)S(1)} collective-permute-done((f32[8,160,128]{2,1,0:T(8,128)S(1)}, f32[8,160,128]{2,1,0:T(8,128)S(1)}, u32[]{:S(2)}, u32[]{:S(2)}) %collective-permute-start) | collective-permute-done | bytes 655392 | tf_op jit(solution)/shard_map/ppermute | solution.py:347
  6.2 0.8 slice_add_fusion
  7.0 12.9 %all-to-all-start = ((f32[32,5,4,128]{3,2,1,0:T(4,128)}), f32[32,5,4,128]{3,2,1,0:T(4,128)S(1)}, u32[]{:S(2)}, u32[]{:S(2)}) async-start(f32[32,5,4,128]{3,2,1,0:T(4,128)} %bitcast.2), calls=%async_computation | async-start | bytes 655360 | tf_op jit(solution)/shard_map/all_to_all | solution.py:343
  19.9 0.0 copy-done
  19.9 0.0 copy-done.3
  19.9 0.0 copy-done.4
  19.9 0.0 copy-start.2
  19.9 5.5 %intra.1 = (bf16[16,256,160]{2,1,0:T(8,128)(2,1)}, f32[256,1024]{1,0:T(8,128)}, f32[256,1024]{1,0:T(8,128)}) custom-call(s32[1]{0:T(128)} %bitcast.core_ref, bf16[256,256]{1,0:T(8,128)(2,1)S(1)} %copy-done.4, bf16[256,256]{1,0:T(8,128)(2,1)S(1)} %copy-done.3, bf16[256,1024]{1,0:T(8,128)(2,1)S(1)} %copy-done, f32[8,160,128]{2,1,0:T(8,128)S(1)} %collective-permute-done.sib_ref), custom_call_target="tpu_custom_call" | custom-call | flops 2000000000 | bytes 16000000 | tf_op jit(solution)/shard_map/intra/pallas_call | solution.py:285
  25.5 4.9 %all-to-all-done = f32[32,5,4,128]{3,2,1,0:T(4,128)S(1)} async-done(((f32[32,5,4,128]{3,2,1,0:T(4,128)}), f32[32,5,4,128]{3,2,1,0:T(4,128)S(1)}, u32[]{:S(2)}, u32[]{:S(2)}) %all-to-all-start) | async-done | bytes 327712 | tf_op jit(solution)/shard_map/all_to_all | solution.py:343
  30.4 0.1 reduce_sum.9
  30.4 0.6 broadcast_in_dim.3
  31.1 6.6 %all-to-all-start.1 = ((f32[8,5,4,128]{3,2,1,0:T(4,128)}), f32[8,5,4,128]{3,2,1,0:T(4,128)S(1)}, u32[]{:S(2)}, u32[]{:S(2)}) async-start(f32[8,5,4,128]{3,2,1,0:T(4,128)} %broadcast_in_dim.3), calls=%async_computation.1 | async-start | bytes 163840 | tf_op jit(solution)/shard_map/all_to_all | solution.py:343
  37.7 0.0 copy-done.2
  37.7 7.9 %collective-permute-start.1 = (bf16[256,1024]{1,0:T(8,128)(2,1)S(1)}, bf16[256,1024]{1,0:T(8,128)(2,1)S(1)}, u32[]{:S(2)}, u32[]{:S(2)}) collective-permute-start(bf16[256,1024]{1,0:T(8,128)(2,1)S(1)} %copy-done.2), channel_id=1, source_target_pairs={{0,1},{1,2},{2,3},{3,4},{4,5},{5,6},{6,7},{7,8},{8,9},{9,10},{10,1... | collective-permute-start | bytes 1572872 | tf_op jit(solution)/shard_map/ppermute | solution.py:374
  45.7 1.9 %collective-permute-start.2 = (bf16[256,1024]{1,0:T(8,128)(2,1)S(1)}, bf16[256,1024]{1,0:T(8,128)(2,1)}, u32[]{:S(2)}, u32[]{:S(2)}) collective-permute-start(bf16[256,1024]{1,0:T(8,128)(2,1)S(1)} %copy-done), channel_id=1, source_target_pairs={{0,1},{1,2},{2,3},{3,4},{4,5},{5,6},{6,7},{7,8},{8,9},{9,10},{10,1... | collective-permute-start | bytes 1572872 | tf_op jit(solution)/shard_map/ppermute | solution.py:375
  47.6 0.0 copy-start.1
  47.6 0.0 all-to-all-done.1
  47.7 0.8 spread.1
  48.4 4.7 %all-to-all-start.2 = ((f32[32,5,4,128]{3,2,1,0:T(4,128)}), f32[32,5,4,128]{3,2,1,0:T(4,128)S(1)}, u32[]{:S(2)}, u32[]{:S(2)}) async-start(f32[32,5,4,128]{3,2,1,0:T(4,128)} %bitcast.5), calls=%async_computation.2 | async-start | bytes 655360 | tf_op jit(solution)/shard_map/all_to_all | solution.py:343
  53.2 0.0 collective-permute-done.1.hk_ref
  53.2 7.5 %collective-permute-done.2.hv_ref = bf16[256,1024]{1,0:T(8,128)(2,1)} collective-permute-done((bf16[256,1024]{1,0:T(8,128)(2,1)S(1)}, bf16[256,1024]{1,0:T(8,128)(2,1)}, u32[]{:S(2)}, u32[]{:S(2)}) %collective-permute-start.2) | collective-permute-done | bytes 524320 | tf_op jit(solution)/shard_map/ppermute | solution.py:375
  60.7 0.0 copy-done.1
  60.7 5.2 %window.1.win_hbm = f32[256,1024]{1,0:T(8,128)} custom-call(s32[1]{0:T(128)} %bitcast.6.start_ref, bf16[256,1024]{1,0:T(8,128)(2,1)S(1)} %copy-done.1, bf16[256,1024]{1,0:T(8,128)(2,1)S(1)} %copy-done.2, bf16[256,1024]{1,0:T(8,128)(2,1)S(1)} %copy-done, bf16[256,1024]{1,0:T(8,128)(2,1)S(1)} %collective-permute-done.1.hk_ref, ...), custom_call_target="tpu_custom_call" | custom-call | flops 2000000000 | bytes 16000000 | tf_op jit(solution)/shard_map/window/pallas_call | solution.py:285
  65.9 2.3 %all-to-all-done.2 = f32[32,5,4,128]{3,2,1,0:T(4,128)S(1)} async-done(((f32[32,5,4,128]{3,2,1,0:T(4,128)}), f32[32,5,4,128]{3,2,1,0:T(4,128)S(1)}, u32[]{:S(2)}, u32[]{:S(2)}) %all-to-all-start.2) | async-done | bytes 327712 | tf_op jit(solution)/shard_map/all_to_all | solution.py:343
  68.2 5.2 %collective-permute-start.3 = (f32[4,160,128]{2,1,0:T(8,128)S(1)}, f32[4,160,128]{2,1,0:T(8,128)S(1)}, u32[]{:S(2)}, u32[]{:S(2)}) collective-permute-start(f32[4,160,128]{2,1,0:T(8,128)S(1)} %bitcast.10), channel_id=1, source_target_pairs={{0,1},{1,0},{2,3},{3,2},{4,5},{5,4},{6,7},{7,6},{8,9},{9,8},{10,11... | collective-permute-start | bytes 983048 | tf_op jit(solution)/shard_map/ppermute | solution.py:347
  73.4 1.2 %collective-permute-done.3.other_ref = f32[4,160,128]{2,1,0:T(8,128)S(1)} collective-permute-done((f32[4,160,128]{2,1,0:T(8,128)S(1)}, f32[4,160,128]{2,1,0:T(8,128)S(1)}, u32[]{:S(2)}, u32[]{:S(2)}) %collective-permute-start.3) | collective-permute-done | bytes 327712 | tf_op jit(solution)/shard_map/ppermute | solution.py:347
  74.7 4.6 %final.1 = bf16[256,1024]{1,0:T(8,128)(2,1)} custom-call(s32[1]{0:T(128)} %bitcast.core_ref, f32[4,160,128]{2,1,0:T(8,128)S(1)} %bitcast.11, f32[4,160,128]{2,1,0:T(8,128)S(1)} %collective-permute-done.3.other_ref, bf16[16,256,160]{2,1,0:T(8,128)(2,1)} %get-tuple-element.41.qf_hbm, f32[256,1024]{1,0:T(8,128)} %get-tuple-element.42.num_hbm, ...), custom_call_target="tpu_custom_call" | custom-call | flops 2000000000 | bytes 10000000 | tf_op jit(solution)/shard_map/final/pallas_call | solution.py:285
  (1 shorter events, 0.0 us)
Async XLA Ops:
  0.0 19.9 %copy-start = (bf16[256,1024]{1,0:T(8,128)(2,1)S(1)}, bf16[256,1024]{1,0:T(8,128)(2,1)}, u32[]{:S(2)}) copy-start(bf16[256,1024]{1,0:T(8,128)(2,1)} %v_ref.3) | copy-start | bytes 1572868
  0.0 19.9 %copy-start.3 = (bf16[256,256]{1,0:T(8,128)(2,1)S(1)}, bf16[256,256]{1,0:T(8,128)(2,1)}, u32[]{:S(2)}) copy-start(bf16[256,256]{1,0:T(8,128)(2,1)} %fk_ref) | copy-start | bytes 393220
  0.0 19.9 %copy-start.4 = (bf16[256,256]{1,0:T(8,128)(2,1)S(1)}, bf16[256,256]{1,0:T(8,128)(2,1)}, u32[]{:S(2)}) copy-start(bf16[256,256]{1,0:T(8,128)(2,1)} %fq_ref) | copy-start | bytes 393220
  1.9 4.3 %collective-permute-start = (f32[8,160,128]{2,1,0:T(8,128)S(1)}, f32[8,160,128]{2,1,0:T(8,128)S(1)}, u32[]{:S(2)}, u32[]{:S(2)}) collective-permute-start(f32[8,160,128]{2,1,0:T(8,128)S(1)} %state.1), channel_id=1, source_target_pairs={{0,1},{1,0},{2,3},{3,2},{4,5},{5,4},{6,7},{7,6},{8,9},{9,8},{10,11... | collective-permute-start | bytes 1966088 | tf_op jit(solution)/shard_map/ppermute | solution.py:347
  7.0 23.4 %all-to-all-start = ((f32[32,5,4,128]{3,2,1,0:T(4,128)}), f32[32,5,4,128]{3,2,1,0:T(4,128)S(1)}, u32[]{:S(2)}, u32[]{:S(2)}) async-start(f32[32,5,4,128]{3,2,1,0:T(4,128)} %bitcast.2), calls=%async_computation | async-start | bytes 655360 | tf_op jit(solution)/shard_map/all_to_all | solution.py:343
  19.9 17.8 %copy-start.2 = (bf16[256,1024]{1,0:T(8,128)(2,1)S(1)}, bf16[256,1024]{1,0:T(8,128)(2,1)}, u32[]{:S(2)}) copy-start(bf16[256,1024]{1,0:T(8,128)(2,1)} %k_ref.1) | copy-start | bytes 1572868
  31.1 16.6 %all-to-all-start.1 = ((f32[8,5,4,128]{3,2,1,0:T(4,128)}), f32[8,5,4,128]{3,2,1,0:T(4,128)S(1)}, u32[]{:S(2)}, u32[]{:S(2)}) async-start(f32[8,5,4,128]{3,2,1,0:T(4,128)} %broadcast_in_dim.3), calls=%async_computation.1 | async-start | bytes 163840 | tf_op jit(solution)/shard_map/all_to_all | solution.py:343
  37.7 15.4 %collective-permute-start.1 = (bf16[256,1024]{1,0:T(8,128)(2,1)S(1)}, bf16[256,1024]{1,0:T(8,128)(2,1)S(1)}, u32[]{:S(2)}, u32[]{:S(2)}) collective-permute-start(bf16[256,1024]{1,0:T(8,128)(2,1)S(1)} %copy-done.2), channel_id=1, source_target_pairs={{0,1},{1,2},{2,3},{3,4},{4,5},{5,6},{6,7},{7,8},{8,9},{9,10},{10,1... | collective-permute-start | bytes 1572872 | tf_op jit(solution)/shard_map/ppermute | solution.py:374
  45.7 15.0 %collective-permute-start.2 = (bf16[256,1024]{1,0:T(8,128)(2,1)S(1)}, bf16[256,1024]{1,0:T(8,128)(2,1)}, u32[]{:S(2)}, u32[]{:S(2)}) collective-permute-start(bf16[256,1024]{1,0:T(8,128)(2,1)S(1)} %copy-done), channel_id=1, source_target_pairs={{0,1},{1,2},{2,3},{3,4},{4,5},{5,6},{6,7},{7,8},{8,9},{9,10},{10,1... | collective-permute-start | bytes 1572872 | tf_op jit(solution)/shard_map/ppermute | solution.py:375
  47.6 13.1 %copy-start.1 = (bf16[256,1024]{1,0:T(8,128)(2,1)S(1)}, bf16[256,1024]{1,0:T(8,128)(2,1)}, u32[]{:S(2)}) copy-start(bf16[256,1024]{1,0:T(8,128)(2,1)} %q_ref) | copy-start | bytes 1572868
  48.4 19.8 %all-to-all-start.2 = ((f32[32,5,4,128]{3,2,1,0:T(4,128)}), f32[32,5,4,128]{3,2,1,0:T(4,128)S(1)}, u32[]{:S(2)}, u32[]{:S(2)}) async-start(f32[32,5,4,128]{3,2,1,0:T(4,128)} %bitcast.5), calls=%async_computation.2 | async-start | bytes 655360 | tf_op jit(solution)/shard_map/all_to_all | solution.py:343
  68.2 6.5 %collective-permute-start.3 = (f32[4,160,128]{2,1,0:T(8,128)S(1)}, f32[4,160,128]{2,1,0:T(8,128)S(1)}, u32[]{:S(2)}, u32[]{:S(2)}) collective-permute-start(f32[4,160,128]{2,1,0:T(8,128)S(1)} %bitcast.10), channel_id=1, source_target_pairs={{0,1},{1,0},{2,3},{3,2},{4,5},{5,4},{6,7},{7,6},{8,9},{9,8},{10,11... | collective-permute-start | bytes 983048 | tf_op jit(solution)/shard_map/ppermute | solution.py:347

commit v2 on v1

--- a/solution.py
+++ b/solution.py
@@ -1,3 +1,5 @@
+import functools
+
 import jax
 import jax.numpy as jnp
 import numpy as np
@@ -11,6 +13,7 @@
 PAIRS = HEADS // 2
 DIM = 16
 ROWS = 256
+QUADS = 4
 FEATS = 153
 FROWS = 160
 PIECES = 32
@@ -118,22 +121,26 @@
     for tail in tails:
         for row in (1, 3):
             rows.append(jnp.concatenate([tail[row : row + 1], tail[row + 1 : row + 2]], 1))
-    rows.append(jnp.zeros((LANES - HEADS, 2 * LANES), F32))
+    rows.append(jnp.zeros((LANES - len(rows), 2 * LANES), F32))
     return jnp.concatenate(rows, 0).T[:FROWS]
 
 
-def cross(qfs, s, zcols, at):
+def laid_out(w, slot):
+    gap = jnp.zeros((32, w.shape[1]), w.dtype)
+    return jnp.concatenate([w[:LANES]] + [gap] * slot + [w[LANES:]] + [gap] * (3 - slot), 0)
+
+
+def cross(qfs, s, zcols, at, slot):
     low, tlow = low_lanes(FROWS), low_lanes(ROWS)
     s = jnp.where(lax.broadcasted_iota(jnp.int32, s.shape, 0) < FEATS, s, F32(0.0))
     res = []
     for h in range(2):
         z = jnp.broadcast_to(zcols[:, at + h : at + h + 1], (FROWS, LANES))
-        hi, mid, lo = split3(jnp.where(low, s, z) if h == 0 else jnp.where(low, z, s))
+        parts = split3(jnp.where(low, s, z) if h == 0 else jnp.where(low, z, s))
+        hi, mid, lo = (laid_out(part, slot + h) for part in parts)
         big = jnp.dot(qfs[h], jnp.concatenate([hi, mid], 1), preferred_element_type=F32)
         res.append(big[:, :LANES] + (big[:, LANES:] + jnp.dot(qfs[h], lo, preferred_element_type=F32)))
-    num = jnp.where(tlow, res[0], res[1])
-    den = pltpu.roll(jnp.where(tlow, res[1], res[0]), 64, 1)
-    return num, den
+    return jnp.where(tlow, res[0], res[1]), jnp.where(tlow, res[1], res[0])
 
 
 def intra_kernel(core_ref, fq_ref, fk_ref, v_ref, sib_ref, qf_hbm, num_hbm, den_hbm, qt_ref, kt_ref, qf_ref, num_ref, den_ref, sems):
@@ -141,21 +148,35 @@
     qt_ref[...] = fq_ref[...].astype(F32).T
     kt_ref[...] = fk_ref[...].astype(F32).T
     low = low_lanes(ROWS)
+    lane = lax.broadcasted_iota(jnp.int32, (ROWS, LANES), 1)
     causal = lax.broadcasted_iota(jnp.int32, (ROWS, ROWS), 0) >= lax.broadcasted_iota(
         jnp.int32, (ROWS, ROWS), 1
     )
     zcols = norm_columns([sib_ref[i, TAIL] for i in range(PAIRS)])
     zcols = jnp.where(second, zcols, F32(0.0))
+    all_dens = jnp.zeros((ROWS, LANES), F32)
     copies = []
-    for quad in range(PAIRS // 2):
-        dens, rounded, qfs = [], [], []
+
+    def send(src, dst, k, quad):
+        copy = pltpu.make_async_copy(src, dst, sems.at[k, quad])
+        copy.start()
+        copies.append(copy)
+
+    for quad in range(QUADS):
+        dens, rounded, mains, rests = [], [], [], []
         for h in range(4 * quad, 4 * quad + 4):
-            rows = slice(h * DIM, (h + 1) * DIM)
-            qf = features(qt_ref[rows, :]).T.astype(BF16)
-            kf = features(kt_ref[rows, :]).astype(BF16)
-            qf_ref[h] = qf
-            qfs.append(qf)
-            a = jnp.dot(qf, kf, preferred_element_type=F32)
+            f = features(qt_ref[h * DIM : (h + 1) * DIM, :])
+            main = f[:LANES].T.astype(BF16)
+            qf_ref[h] = main
+            mains.append(main)
+            rests.append(f[LANES:])
+        rest = jnp.concatenate(rests, 0).T.astype(BF16)
+        qf_ref[HEADS + quad] = rest
+        qfs = [jnp.concatenate([main, rest], 1) for main in mains]
+        for slot in range(4):
+            h = 4 * quad + slot
+            kf = laid_out(features(kt_ref[h * DIM : (h + 1) * DIM, :]).astype(BF16), slot)
+            a = jnp.dot(qfs[slot], kf, preferred_element_type=F32)
             a = jnp.where(causal, a, F32(0.0))
             dens.append(jnp.sum(a, -1, keepdims=True))
             rounded.append(a.astype(BF16))
@@ -164,25 +185,20 @@
         for p in range(2):
             pair = 2 * quad + p
             s = jnp.where(second, sib_ref[pair], F32(0.0))
-            num, den = cross(qfs[2 * p : 2 * p + 2], s, zcols, 2 * pair)
-            lanes = slice(pair * LANES, (pair + 1) * LANES)
+            num, den = cross(qfs[2 * p : 2 * p + 2], s, zcols, 2 * pair, 2 * p)
             here = slice(p * LANES, (p + 1) * LANES)
             n0 = nums[2 * p * ROWS : (2 * p + 1) * ROWS, here]
             n1 = nums[(2 * p + 1) * ROWS : (2 * p + 2) * ROWS, here]
-            num_ref[:, lanes] = num + jnp.where(low, n0, n1)
-            den_ref[:, lanes] = den + jnp.where(low, dens[2 * p], dens[2 * p + 1])
+            num_ref[quad, :, here] = num + jnp.where(low, n0, n1)
+            den = den + jnp.where(low, dens[2 * p + 1], dens[2 * p])
+            place = jnp.where(second, (pair + PAIRS // 2) % PAIRS, pair)
+            all_dens = jnp.where(lane % 64 == place, den, all_dens)
         heads = pl.ds(4 * quad, 4)
-        lanes = pl.ds(quad * 256, 256)
-        for k, (src, dst) in enumerate(
-            (
-                (qf_ref.at[heads], qf_hbm.at[heads]),
-                (num_ref.at[:, lanes], num_hbm.at[:, lanes]),
-                (den_ref.at[:, lanes], den_hbm.at[:, lanes]),
-            )
-        ):
-            copy = pltpu.make_async_copy(src, dst, sems.at[k, quad])
-            copy.start()
-            copies.append(copy)
+        send(qf_ref.at[heads], qf_hbm.at[heads], 0, quad)
+        send(qf_ref.at[pl.ds(HEADS + quad, 1)], qf_hbm.at[pl.ds(HEADS + quad, 1)], 1, quad)
+        send(num_ref.at[quad], num_hbm.at[quad], 2, quad)
+    den_ref[...] = all_dens
+    send(den_ref, den_hbm, 3, 0)
     for copy in copies:
         copy.wait()
 
@@ -223,61 +239,97 @@
             res = o[:half]
             for h in range(1, 4):
                 res = jnp.where(head == h, o[h * half : (h + 1) * half], res)
-            out_ref[mine, lanes] = res
-        at = pl.ds(quad * 256, 256)
-        copy = pltpu.make_async_copy(out_ref.at[:, at], out_hbm.at[:, at], sems.at[quad])
+            out_ref[quad, mine] = res
+        copy = pltpu.make_async_copy(out_ref.at[quad], out_hbm.at[quad], sems.at[quad])
         copy.start()
         copies.append(copy)
     for copy in copies:
         copy.wait()
 
 
-def final_kernel(core_ref, mine_ref, other_ref, qf_hbm, num_hbm, den_hbm, win_hbm, out_ref, qf_ref, num_ref, den_ref, win_ref, sems):
-    first = core_ref[0] * (PAIRS // 2)
-    half = PAIRS // 2
-    copies = []
-    for i in range(4):
-        quad = lax.rem(core_ref[0] * 2 + i, 4)
-        heads = pl.ds(4 * quad, 4)
-        lanes = pl.ds(pl.multiple_of(quad * 256, 256), 256)
+def finish(part, p_ref, qf_ref, num_ref, den_ref, win_ref, out_ref, q, zcols):
+    low = low_lanes(ROWS)
+    rest = qf_ref[8 + q]
+    for p in range(2):
+        i = 2 * q + p
+        qfs = [jnp.concatenate([qf_ref[2 * i + h], rest], 1) for h in range(2)]
+        num, den = cross(qfs, p_ref[i], zcols, 2 * i, 2 * p)
+        at = PAIRS // 2 * part + i
+        den = den + jnp.where(low, den_ref[:, at : at + 1], den_ref[:, 64 + at : 65 + at])
+        here = slice(p * LANES, (p + 1) * LANES)
+        linear = (num + num_ref[q, :, here]) / pltpu.roll(den, 64, 1)
+        out_ref[q, :, here] = (linear + win_ref[q, :, here]).astype(BF16)
+
+
+def norms_of(p_ref):
+    return norm_columns([p_ref[i, TAIL] for i in range(PAIRS // 2)])
+
+
+def leave(out_ref, out_hbm, half, q, sems):
+    lanes = pl.ds(pl.multiple_of(half * 512 + q * 256, 256), 256)
+    copy = pltpu.make_async_copy(out_ref.at[q], out_hbm.at[:, lanes], sems.at[q])
+    copy.start()
+    return copy
+
+
+def first_kernel(
+    core_ref, p_ref, qf_hbm, num_hbm, den_hbm, win_hbm, out_hbm, qf2_ref, num2_ref, den_ref, win2_ref,
+    qf_ref, num_ref, win_ref, out_ref, sems, out_sems,
+):
+    core = core_ref[0]
+    dens = pltpu.make_async_copy(den_hbm, den_ref, sems.at[2, 0])
+    dens.start()
+    groups = []
+    for part, half in ((0, core), (1, 1 - core)):
+        to = ((qf_ref, num_ref, win_ref), (qf2_ref, num2_ref, win2_ref))[part]
+        two = pl.ds(2 * half, 2)
         group = []
         for k, (src, dst) in enumerate(
             (
-                (qf_hbm.at[heads], qf_ref.at[heads]),
-                (num_hbm.at[:, lanes], num_ref.at[:, lanes]),
-                (den_hbm.at[:, lanes], den_ref.at[:, lanes]),
-                (win_hbm.at[:, lanes], win_ref.at[:, lanes]),
+                (qf_hbm.at[pl.ds(8 * half, 8)], to[0].at[pl.ds(0, 8)]),
+                (qf_hbm.at[pl.ds(HEADS + 2 * half, 2)], to[0].at[pl.ds(8, 2)]),
+                (num_hbm.at[two], to[1]),
+                (win_hbm.at[two], to[2]),
             )
         ):
-            copy = pltpu.make_async_copy(src, dst, sems.at[k, i])
+            copy = pltpu.make_async_copy(src, dst, sems.at[part, k])
             copy.start()
             group.append(copy)
-        copies.append(group)
-    refs = [mine_ref] * half + [other_ref] * half
-    zcols = norm_columns([refs[i][i % half, TAIL] for i in range(PAIRS)])
-    for i in range(PAIRS):
-        if i % 2 == 0:
-            for copy in copies[i // 2]:
-                copy.wait()
-        pair = lax.rem(first + i, PAIRS)
-        lanes = pl.ds(pl.multiple_of(pair * LANES, LANES), LANES)
-        qfs = [qf_ref[pair * 2], qf_ref[pair * 2 + 1]]
-        num, den = cross(qfs, refs[i][i % half], zcols, 2 * i)
-        linear = (num + num_ref[:, lanes]) / (den + den_ref[:, lanes])
-        out_ref[:, lanes] = (linear + win_ref[:, lanes]).astype(BF16)
+        groups.append(group)
+    zcols = norms_of(p_ref)
+    dens.wait()
+    for copy in groups[0]:
+        copy.wait()
+    leaving = []
+    for q in range(2):
+        finish(0, p_ref, qf_ref, num_ref, den_ref, win_ref, out_ref, q, zcols)
+        leaving.append(leave(out_ref, out_hbm, core, q, out_sems))
+    for copy in groups[1] + leaving:
+        copy.wait()
+
+
+def second_kernel(core_ref, p_ref, qf_ref, num_ref, den_ref, win_ref, done_hbm, out_hbm, out_ref, out_sems):
+    zcols = norms_of(p_ref)
+    leaving = []
+    for q in range(2):
+        finish(1, p_ref, qf_ref, num_ref, den_ref, win_ref, out_ref, q, zcols)
+        leaving.append(leave(out_ref, out_hbm, 1 - core_ref[0], q, out_sems))
+    for copy in leaving:
+        copy.wait()
 
 
 def spec(kind=pltpu.VMEM):
     return pl.BlockSpec(memory_space=kind)
 
 
-def call(kernel, ins, outs, scratch, flops, moved, name):
+def call(kernel, ins, outs, scratch, flops, moved, name, aliases={}):
     made = pl.pallas_call(
         kernel,
         out_shape=[pltpu.HBM(o.shape, o.dtype) if k == HB else o for o, k in outs],
         in_specs=[spec(k) for k in ins],
         out_specs=[spec(k) for _, k in outs],
         scratch_shapes=scratch,
+        input_output_aliases=aliases,
         compiler_params=pltpu.CompilerParams(vmem_limit_bytes=40 * 2**20),
         cost_estimate=pl.CostEstimate(flops=flops, bytes_accessed=moved, transcendentals=0),
         name=name,
@@ -293,8 +345,12 @@
 
 SM, VM, HB = pltpu.SMEM, pltpu.VMEM, pltpu.HBM
 TURNED = pltpu.VMEM((256, ROWS), F32)
-WIDE = pltpu.VMEM((ROWS, VALUES), F32)
-QF = (HEADS, ROWS, FROWS)
+WIDE = pltpu.VMEM((QUADS, ROWS, 256), F32)
+QF = (HEADS + QUADS, ROWS, LANES)
+DENS = (ROWS, LANES)
+BY_QUADS = (QUADS, ROWS, 256)
+HALF_QF = (10, ROWS, LANES)
+HALF = (2, ROWS, 256)
 
 
 def own_state(core, fk, v):
@@ -317,26 +373,39 @@
 
 
 def intra(core, fq, fk, v, sib):
-    wide = shape(ROWS, VALUES)
     return call(
-        intra_kernel, [SM, VM, VM, VM, VM], [(shape(*QF, dtype=BF16), HB), (wide, HB), (wide, HB)],
-        [TURNED, TURNED, pltpu.VMEM(QF, BF16), WIDE, WIDE, pltpu.SemaphoreType.DMA((3, 4))],
-        2000000000, 16 * 10**6, "intra",
+        intra_kernel, [SM, VM, VM, VM, VM],
+        [(shape(*QF, dtype=BF16), HB), (shape(*BY_QUADS), HB), (shape(*DENS), HB)],
+        [TURNED, TURNED, pltpu.VMEM(QF, BF16), WIDE, pltpu.VMEM(DENS, F32), pltpu.SemaphoreType.DMA((4, 4))],
+        2 * 10**9, 16 * 10**6, "intra",
     )(core, fq, fk, v, sib)
 
 
 def window(start, q, k, v, hk, hv):
     return call(
-        window_kernel, [SM] + [VM] * 5, [(shape(ROWS, VALUES), HB)], [WIDE, pltpu.SemaphoreType.DMA((4,))],
+        window_kernel, [SM] + [VM] * 5, [(shape(*BY_QUADS), HB)], [WIDE, pltpu.SemaphoreType.DMA((4,))],
         2 * 10**9, 16 * 10**6, "window",
     )(start, q, k, v, hk, hv)[0]
 
 
-def final(core, mine, other, qf, num, den, win):
+OUT = (shape(ROWS, VALUES, dtype=BF16), HB)
+OUT_SCRATCH = [pltpu.VMEM(HALF, BF16), pltpu.SemaphoreType.DMA((2,))]
+
+
+def final_first(core, prior, qf, num, den, win):
     return call(
-        final_kernel, [SM, VM, VM] + [HB] * 4, [(shape(ROWS, VALUES, dtype=BF16), VM)],
-        [pltpu.VMEM(QF, BF16), WIDE, WIDE, WIDE, pltpu.SemaphoreType.DMA((4, 4))], 2 * 10**9, 10**7, "final",
-    )(core, mine, other, qf, num, den, win)[0]
+        first_kernel, [SM, VM] + [HB] * 4,
+        [OUT, (shape(*HALF_QF, dtype=BF16), VM), (shape(*HALF), VM), (shape(*DENS), VM), (shape(*HALF), VM)],
+        [pltpu.VMEM(HALF_QF, BF16), pltpu.VMEM(HALF, F32), pltpu.VMEM(HALF, F32), OUT_SCRATCH[0],
+         pltpu.SemaphoreType.DMA((3, 4)), OUT_SCRATCH[1]],
+        2 * 10**9, 10**7, "first",
+    )(core, prior, qf, num, den, win)
+
+
+def final_second(core, prior, qf, num, den, win, done):
+    return call(
+        second_kernel, [SM] + [VM] * 5 + [HB], [OUT], OUT_SCRATCH, 2 * 10**9, 10**6, "second", {6: 0}
+    )(core, prior, qf, num, den, win, done)[0]
 
 
 def exchange(array, axes):
@@ -365,14 +434,15 @@
     chip, fq, fk = after(chip, fq, fk)
     pieces = exchange(chip, ("x", "z"))
     qf, num, den = intra(core, fq, fk, v, sib)
+    count = lax.axis_size(AXES)
+    pairs = [(i, i + 1) for i in range(count - 1)]
+    qf, wk_out, v_out = after(qf, wk, v)
+    hk = lax.ppermute(wk_out, AXES, pairs)
+    hv = lax.ppermute(v_out, AXES, pairs)
     pieces, qf, num, den = after(pieces, qf, num, den)
     total = jnp.broadcast_to(jnp.sum(pieces, 0), (8, *PIECE))
-    total, pieces, wk_out, v_out = after(total, pieces, wk, v)
+    total, pieces = after(total, pieces)
     rows = exchange(total, "y")
-    count = lax.axis_size(AXES)
-    pairs = [(i, i + 1) for i in range(count - 1)]
-    hk = lax.ppermute(wk_out, AXES, pairs)
-    hv = lax.ppermute(v_out, AXES, pairs)
     before = inner(pieces)
     rows, before = after(rows, before)
     back = spread(scalar(lax.axis_index("y")), before, rows)
@@ -382,7 +452,8 @@
     mine, win = after(mine, win)
     mine = mine.reshape(half, PAIR_ROWS, LANES)
     other = swap(mine)
-    return final(core, mine, other, qf, num, den, win)
+    done, *rest = final_first(core, mine, qf, num, den, win)
+    return final_second(core, other, *rest, done)
 
 
 def solution(mesh):

time: 79.8 us -> 76.5 us (0.959)
  the two profiles are of different devices: /device:TPU:33 before, /device:TPU:1 now
where the time goes in v2:
time: 76.5 us; the launch traced here: 76 us
  starting transfers between devices  43.3 us (57%)
  Pallas kernels  16.8 us (22%)
  waiting for transfers between devices  14.2 us (19%)
  other arithmetic  0.84 us (1%)
    all_to_all x3, starting transfers between devices, exchange(): return lax.all_to_all(array, axes, split_axis=0, concat_axis=0, tiled=True)  22.2 us
    pallas_call x7, Pallas kernels, call(): made(*(pltpu.with_memory_space_constraint(a, k) if k == HB else a for a,...  16.8 us
    ppermute x2, starting transfers between devices, swap(): return lax.ppermute(array, 'c', [(0, 1), (1, 0)])  15.2 us
    all_to_all x3, waiting for transfers between devices, exchange(): return lax.all_to_all(array, axes, split_axis=0, concat_axis=0, tiled=True)  12.5 us
    ppermute x1, starting transfers between devices, body(): hk = lax.ppermute(wk_out, AXES, pairs)  3.96 us
    ppermute x1, starting transfers between devices, body(): hv = lax.ppermute(v_out, AXES, pairs)  1.92 us
    ppermute x2, waiting for transfers between devices, swap(): return lax.ppermute(array, 'c', [(0, 1), (1, 0)])  1.7 us
  transfers between devices with their start and end apart: 7, of which 4 were waited for; matrix products, arithmetic and copies ran while one was open for 1% of the time, Pallas kernels for 17%

profile of v2, /device:TPU:1, one launch (start us, length us, event | category | flops | bytes accessed | tf_op | source)
XLA Modules:
  0.0 76.0 jit_solution(2349097205457630205)
XLA Ops:
  0.0 1.8 %state.1 = f32[8,160,128]{2,1,0:T(8,128)S(1)} custom-call(s32[1]{0:T(128)} %bitcast.core_ref, bf16[256,256]{1,0:T(8,128)(2,1)} %fk_ref, bf16[256,1024]{1,0:T(8,128)(2,1)} %v_ref.3), custom_call_target="tpu_custom_call" | custom-call | flops 1000000000 | bytes 5000000 | tf_op jit(solution)/shard_map/state/pallas_call | solution.py:337
  1.9 0.0 copy-start
  1.9 0.0 copy-start.3
  1.9 0.0 copy-start.4
  1.9 8.9 %collective-permute-start = (f32[8,160,128]{2,1,0:T(8,128)S(1)}, f32[8,160,128]{2,1,0:T(8,128)S(1)}, u32[]{:S(2)}, u32[]{:S(2)}) collective-permute-start(f32[8,160,128]{2,1,0:T(8,128)S(1)} %state.1), channel_id=1, source_target_pairs={{0,1},{1,0},{2,3},{3,2},{4,5},{5,4},{6,7},{7,6},{8,9},{9,8},{10,11... | collective-permute-start | bytes 1966088 | tf_op jit(solution)/shard_map/ppermute | solution.py:416
  10.8 1.7 %collective-permute-done.sib_ref = f32[8,160,128]{2,1,0:T(8,128)S(1)} collective-permute-done((f32[8,160,128]{2,1,0:T(8,128)S(1)}, f32[8,160,128]{2,1,0:T(8,128)S(1)}, u32[]{:S(2)}, u32[]{:S(2)}) %collective-permute-start) | collective-permute-done | bytes 655392 | tf_op jit(solution)/shard_map/ppermute | solution.py:416
  12.5 0.8 %slice_add_fusion = f32[4,160,128]{2,1,0:T(8,128)} fusion(f32[8,160,128]{2,1,0:T(8,128)S(1)} %collective-permute-done.sib_ref, f32[8,160,128]{2,1,0:T(8,128)S(1)} %state.1), kind=kLoop, calls=%fused_computation | loop fusion | flops 81920 | bytes 983040 | tf_op jit(solution)/shard_map/add | solution.py:433
  13.3 7.5 %all-to-all-start = ((f32[32,5,4,128]{3,2,1,0:T(4,128)}), f32[32,5,4,128]{3,2,1,0:T(4,128)S(1)}, u32[]{:S(2)}, u32[]{:S(2)}) async-start(f32[32,5,4,128]{3,2,1,0:T(4,128)} %bitcast.2), calls=%async_computation | async-start | bytes 655360 | tf_op jit(solution)/shard_map/all_to_all | solution.py:412
  20.8 0.0 copy-done
  20.8 0.0 copy-done.3
  20.8 0.0 copy-done.4
  20.9 0.0 copy-start.2
  20.9 4.1 %intra.1 = (bf16[20,256,128]{2,1,0:T(8,128)(2,1)}, f32[4,256,256]{2,1,0:T(8,128)}, f32[256,128]{1,0:T(8,128)}) custom-call(s32[1]{0:T(128)} %bitcast.core_ref, bf16[256,256]{1,0:T(8,128)(2,1)S(1)} %copy-done.4, bf16[256,256]{1,0:T(8,128)(2,1)S(1)} %copy-done.3, bf16[256,1024]{1,0:T(8,128)(2,1)S(1)} %copy-done, f32[8,160,128]{2,1,0:T(8,128)S(1)} %collective-permute-done.sib_ref), custom_call_target="tpu_custom_call" | custom-call | flops 2000000000 | bytes 16000000 | tf_op jit(solution)/shard_map/intra/pallas_call | solution.py:337
  25.0 0.0 copy-done.2
  25.0 4.0 %collective-permute-start.1 = (bf16[256,1024]{1,0:T(8,128)(2,1)S(1)}, bf16[256,1024]{1,0:T(8,128)(2,1)S(1)}, u32[]{:S(2)}, u32[]{:S(2)}) collective-permute-start(bf16[256,1024]{1,0:T(8,128)(2,1)S(1)} %copy-done.2), channel_id=1, source_target_pairs={{0,1},{1,2},{2,3},{3,4},{4,5},{5,6},{6,7},{7,8},{8,9},{9,10},{10,1... | collective-permute-start | bytes 1572872 | tf_op jit(solution)/shard_map/ppermute | solution.py:440
  29.0 1.9 %collective-permute-start.2 = (bf16[256,1024]{1,0:T(8,128)(2,1)S(1)}, bf16[256,1024]{1,0:T(8,128)(2,1)}, u32[]{:S(2)}, u32[]{:S(2)}) collective-permute-start(bf16[256,1024]{1,0:T(8,128)(2,1)S(1)} %copy-done), channel_id=1, source_target_pairs={{0,1},{1,2},{2,3},{3,4},{4,5},{5,6},{6,7},{7,8},{8,9},{9,10},{10,1... | collective-permute-start | bytes 1572872 | tf_op jit(solution)/shard_map/ppermute | solution.py:441
  30.9 0.4 all-to-all-done
  31.3 0.1 reduce_sum.9
  31.4 0.6 broadcast_in_dim.3
  32.0 6.8 %all-to-all-start.1 = ((f32[8,5,4,128]{3,2,1,0:T(4,128)}), f32[8,5,4,128]{3,2,1,0:T(4,128)S(1)}, u32[]{:S(2)}, u32[]{:S(2)}) async-start(f32[8,5,4,128]{3,2,1,0:T(4,128)} %broadcast_in_dim.3), calls=%async_computation.1 | async-start | bytes 163840 | tf_op jit(solution)/shard_map/all_to_all | solution.py:412
  38.9 0.0 copy-start.1
  38.9 7.4 %all-to-all-done.1 = f32[8,5,4,128]{3,2,1,0:T(4,128)S(1)} async-done(((f32[8,5,4,128]{3,2,1,0:T(4,128)}), f32[8,5,4,128]{3,2,1,0:T(4,128)S(1)}, u32[]{:S(2)}, u32[]{:S(2)}) %all-to-all-start.1) | async-done | bytes 81952 | tf_op jit(solution)/shard_map/all_to_all | solution.py:412
  46.2 0.8 %spread.1 = f32[640,128]{1,0:T(8,128)} custom-call(s32[1]{0:T(128)} %bitcast.1.y_ref, f32[640,128]{1,0:T(8,128)S(1)} %inner.1.inner_ref, f32[160,128]{1,0:T(8,128)S(1)} %bitcast.9), custom_call_target="tpu_custom_call" | custom-call | flops 1000000 | bytes 1000000 | tf_op jit(solution)/shard_map/spread/pallas_call | solution.py:337
  47.0 7.9 %all-to-all-start.2 = ((f32[32,5,4,128]{3,2,1,0:T(4,128)}), f32[32,5,4,128]{3,2,1,0:T(4,128)S(1)}, u32[]{:S(2)}, u32[]{:S(2)}) async-start(f32[32,5,4,128]{3,2,1,0:T(4,128)} %bitcast.5), calls=%async_computation.2 | async-start | bytes 655360 | tf_op jit(solution)/shard_map/all_to_all | solution.py:412
  54.9 0.0 collective-permute-done.1.hk_ref
  54.9 0.0 collective-permute-done.2.hv_ref
  54.9 0.0 copy-done.1
  54.9 5.2 %window.1.win_hbm = f32[4,256,256]{2,1,0:T(8,128)} custom-call(s32[1]{0:T(128)} %bitcast.6.start_ref, bf16[256,1024]{1,0:T(8,128)(2,1)S(1)} %copy-done.1, bf16[256,1024]{1,0:T(8,128)(2,1)S(1)} %copy-done.2, bf16[256,1024]{1,0:T(8,128)(2,1)S(1)} %copy-done, bf16[256,1024]{1,0:T(8,128)(2,1)S(1)} %collective-permute-done.1.hk_ref, ...), custom_call_target="tpu_custom_call" | custom-call | flops 2000000000 | bytes 16000000 | tf_op jit(solution)/shard_map/window/pallas_call | solution.py:337
  60.1 4.7 %all-to-all-done.2 = f32[32,5,4,128]{3,2,1,0:T(4,128)S(1)} async-done(((f32[32,5,4,128]{3,2,1,0:T(4,128)}), f32[32,5,4,128]{3,2,1,0:T(4,128)S(1)}, u32[]{:S(2)}, u32[]{:S(2)}) %all-to-all-start.2) | async-done | bytes 327712 | tf_op jit(solution)/shard_map/all_to_all | solution.py:412
  64.8 6.3 %collective-permute-start.3 = (f32[4,160,128]{2,1,0:T(8,128)S(1)}, f32[4,160,128]{2,1,0:T(8,128)S(1)}, u32[]{:S(2)}, u32[]{:S(2)}) collective-permute-start(f32[4,160,128]{2,1,0:T(8,128)S(1)} %bitcast.10), channel_id=1, source_target_pairs={{0,1},{1,0},{2,3},{3,2},{4,5},{5,4},{6,7},{7,6},{8,9},{9,8},{10,11... | collective-permute-start | bytes 983048 | tf_op jit(solution)/shard_map/ppermute | solution.py:416
  71.1 3.1 %first.1 = (bf16[256,1024]{1,0:T(8,128)(2,1)}, bf16[10,256,128]{2,1,0:T(8,128)(2,1)S(1)}, f32[2,256,256]{2,1,0:T(8,128)S(1)}, f32[256,128]{1,0:T(8,128)S(1)}, f32[2,256,256]{2,1,0:T(8,128)S(1)}) custom-call(s32[1]{0:T(128)} %bitcast.core_ref, f32[4,160,128]{2,1,0:T(8,128)S(1)} %bitcast.11, bf16[20,256,128]{2,1,0:T(8,128)(2,1)} %get-tuple-element.48.qf_hbm, ...), custom_call_target="tpu_custom_call" | custom-call | flops 2000000000 | bytes 10000000 | tf_op jit(solution)/shard_map/first/pallas_call | solution.py:337
  74.3 0.0 collective-permute-done.3.p_ref
  74.3 1.7 %second.1 = bf16[256,1024]{1,0:T(8,128)(2,1)} custom-call(s32[1]{0:T(128)} %bitcast.core_ref, f32[4,160,128]{2,1,0:T(8,128)S(1)} %collective-permute-done.3.p_ref, bf16[10,256,128]{2,1,0:T(8,128)(2,1)S(1)} %get-tuple-element.52.qf_ref, f32[2,256,256]{2,1,0:T(8,128)S(1)} %get-tuple-element.53.num_ref, ...), custom_call_target="tpu_custom_call", output_to_operand_aliasing={{}: (6, {})} | custom-call | flops 2000000000 | bytes 1000000 | tf_op jit(solution)/shard_map/second/pallas_call | solution.py:337
  (1 shorter events, 0.0 us)
Async XLA Ops:
  1.9 19.0 %copy-start = (bf16[256,1024]{1,0:T(8,128)(2,1)S(1)}, bf16[256,1024]{1,0:T(8,128)(2,1)}, u32[]{:S(2)}) copy-start(bf16[256,1024]{1,0:T(8,128)(2,1)} %v_ref.3) | copy-start | bytes 1572868
  1.9 19.0 %copy-start.3 = (bf16[256,256]{1,0:T(8,128)(2,1)S(1)}, bf16[256,256]{1,0:T(8,128)(2,1)}, u32[]{:S(2)}) copy-start(bf16[256,256]{1,0:T(8,128)(2,1)} %fk_ref) | copy-start | bytes 393220
  1.9 19.0 %copy-start.4 = (bf16[256,256]{1,0:T(8,128)(2,1)S(1)}, bf16[256,256]{1,0:T(8,128)(2,1)}, u32[]{:S(2)}) copy-start(bf16[256,256]{1,0:T(8,128)(2,1)} %fq_ref) | copy-start | bytes 393220
  1.9 10.6 %collective-permute-start = (f32[8,160,128]{2,1,0:T(8,128)S(1)}, f32[8,160,128]{2,1,0:T(8,128)S(1)}, u32[]{:S(2)}, u32[]{:S(2)}) collective-permute-start(f32[8,160,128]{2,1,0:T(8,128)S(1)} %state.1), channel_id=1, source_target_pairs={{0,1},{1,0},{2,3},{3,2},{4,5},{5,4},{6,7},{7,6},{8,9},{9,8},{10,11... | collective-permute-start | bytes 1966088 | tf_op jit(solution)/shard_map/ppermute | solution.py:416
  13.3 18.0 %all-to-all-start = ((f32[32,5,4,128]{3,2,1,0:T(4,128)}), f32[32,5,4,128]{3,2,1,0:T(4,128)S(1)}, u32[]{:S(2)}, u32[]{:S(2)}) async-start(f32[32,5,4,128]{3,2,1,0:T(4,128)} %bitcast.2), calls=%async_computation | async-start | bytes 655360 | tf_op jit(solution)/shard_map/all_to_all | solution.py:412
  20.9 4.1 %copy-start.2 = (bf16[256,1024]{1,0:T(8,128)(2,1)S(1)}, bf16[256,1024]{1,0:T(8,128)(2,1)}, u32[]{:S(2)}) copy-start(bf16[256,1024]{1,0:T(8,128)(2,1)} %k_ref.1) | copy-start | bytes 1572868
  25.0 29.9 %collective-permute-start.1 = (bf16[256,1024]{1,0:T(8,128)(2,1)S(1)}, bf16[256,1024]{1,0:T(8,128)(2,1)S(1)}, u32[]{:S(2)}, u32[]{:S(2)}) collective-permute-start(bf16[256,1024]{1,0:T(8,128)(2,1)S(1)} %copy-done.2), channel_id=1, source_target_pairs={{0,1},{1,2},{2,3},{3,4},{4,5},{5,6},{6,7},{7,8},{8,9},{9,10},{10,1... | collective-permute-start | bytes 1572872 | tf_op jit(solution)/shard_map/ppermute | solution.py:440
  29.0 26.0 %collective-permute-start.2 = (bf16[256,1024]{1,0:T(8,128)(2,1)S(1)}, bf16[256,1024]{1,0:T(8,128)(2,1)}, u32[]{:S(2)}, u32[]{:S(2)}) collective-permute-start(bf16[256,1024]{1,0:T(8,128)(2,1)S(1)} %copy-done), channel_id=1, source_target_pairs={{0,1},{1,2},{2,3},{3,4},{4,5},{5,6},{6,7},{7,8},{8,9},{9,10},{10,1... | collective-permute-start | bytes 1572872 | tf_op jit(solution)/shard_map/ppermute | solution.py:441
  32.0 14.2 %all-to-all-start.1 = ((f32[8,5,4,128]{3,2,1,0:T(4,128)}), f32[8,5,4,128]{3,2,1,0:T(4,128)S(1)}, u32[]{:S(2)}, u32[]{:S(2)}) async-start(f32[8,5,4,128]{3,2,1,0:T(4,128)} %broadcast_in_dim.3), calls=%async_computation.1 | async-start | bytes 163840 | tf_op jit(solution)/shard_map/all_to_all | solution.py:412
  38.9 16.1 %copy-start.1 = (bf16[256,1024]{1,0:T(8,128)(2,1)S(1)}, bf16[256,1024]{1,0:T(8,128)(2,1)}, u32[]{:S(2)}) copy-start(bf16[256,1024]{1,0:T(8,128)(2,1)} %q_ref) | copy-start | bytes 1572868
  47.0 17.9 %all-to-all-start.2 = ((f32[32,5,4,128]{3,2,1,0:T(4,128)}), f32[32,5,4,128]{3,2,1,0:T(4,128)S(1)}, u32[]{:S(2)}, u32[]{:S(2)}) async-start(f32[32,5,4,128]{3,2,1,0:T(4,128)} %bitcast.5), calls=%async_computation.2 | async-start | bytes 655360 | tf_op jit(solution)/shard_map/all_to_all | solution.py:412
  64.8 9.4 %collective-permute-start.3 = (f32[4,160,128]{2,1,0:T(8,128)S(1)}, f32[4,160,128]{2,1,0:T(8,128)S(1)}, u32[]{:S(2)}, u32[]{:S(2)}) collective-permute-start(f32[4,160,128]{2,1,0:T(8,128)S(1)} %bitcast.10), channel_id=1, source_target_pairs={{0,1},{1,0},{2,3},{3,2},{4,5},{5,4},{6,7},{7,6},{8,9},{9,8},{10,11... | collective-permute-start | bytes 983048 | tf_op jit(solution)/shard_map/ppermute | solution.py:416

commit v3 on v2

--- a/solution.py
+++ b/solution.py
@@ -272,48 +272,45 @@
     return copy
 
 
-def first_kernel(
-    core_ref, p_ref, qf_hbm, num_hbm, den_hbm, win_hbm, out_hbm, qf2_ref, num2_ref, den_ref, win2_ref,
-    qf_ref, num_ref, win_ref, out_ref, sems, out_sems,
-):
+def stage_kernel(core_ref, qf_hbm, num_hbm, den_hbm, win_hbm, *refs):
     core = core_ref[0]
-    dens = pltpu.make_async_copy(den_hbm, den_ref, sems.at[2, 0])
-    dens.start()
-    groups = []
-    for part, half in ((0, core), (1, 1 - core)):
-        to = ((qf_ref, num_ref, win_ref), (qf2_ref, num2_ref, win2_ref))[part]
-        two = pl.ds(2 * half, 2)
-        group = []
-        for k, (src, dst) in enumerate(
-            (
-                (qf_hbm.at[pl.ds(8 * half, 8)], to[0].at[pl.ds(0, 8)]),
-                (qf_hbm.at[pl.ds(HEADS + 2 * half, 2)], to[0].at[pl.ds(8, 2)]),
-                (num_hbm.at[two], to[1]),
-                (win_hbm.at[two], to[2]),
-            )
-        ):
-            copy = pltpu.make_async_copy(src, dst, sems.at[part, k])
-            copy.start()
-            group.append(copy)
-        groups.append(group)
+    qf_ref, num_ref, win_ref, qf2_ref, num2_ref, den_ref, sems = refs
+    copies = []
+    for k, (src, dst) in enumerate(
+        (
+            (den_hbm, den_ref),
+            (qf_hbm.at[pl.ds(8 * core, 8)], qf_ref.at[pl.ds(0, 8)]),
+            (qf_hbm.at[pl.ds(HEADS + 2 * core, 2)], qf_ref.at[pl.ds(8, 2)]),
+            (num_hbm.at[pl.ds(2 * core, 2)], num_ref),
+            (qf_hbm.at[pl.ds(8 - 8 * core, 8)], qf2_ref.at[pl.ds(0, 8)]),
+            (qf_hbm.at[pl.ds(HEADS + 2 - 2 * core, 2)], qf2_ref.at[pl.ds(8, 2)]),
+            (num_hbm.at[pl.ds(2 - 2 * core, 2)], num2_ref),
+            (win_hbm.at[pl.ds(2 * core, 2)], win_ref),
+        )
+    ):
+        copies.append(pltpu.make_async_copy(src, dst, sems.at[k]))
+    for copy in copies:
+        copy.start()
+    for copy in copies:
+        copy.wait()
+
+
+def first_kernel(core_ref, p_ref, qf_ref, num_ref, den_ref, win_ref, win_hbm, out_ref, win2_ref, sem):
+    win = pltpu.make_async_copy(win_hbm.at[pl.ds(2 - 2 * core_ref[0], 2)], win2_ref, sem.at[0])
+    win.start()
     zcols = norms_of(p_ref)
-    dens.wait()
-    for copy in groups[0]:
-        copy.wait()
-    leaving = []
     for q in range(2):
         finish(0, p_ref, qf_ref, num_ref, den_ref, win_ref, out_ref, q, zcols)
-        leaving.append(leave(out_ref, out_hbm, core, q, out_sems))
-    for copy in groups[1] + leaving:
-        copy.wait()
-
-
-def second_kernel(core_ref, p_ref, qf_ref, num_ref, den_ref, win_ref, done_hbm, out_hbm, out_ref, out_sems):
+    win.wait()
+
+
+def second_kernel(core_ref, p_ref, qf_ref, num_ref, den_ref, win_ref, done_ref, out_hbm, out_ref, sems):
+    core = core_ref[0]
+    leaving = [leave(done_ref, out_hbm, core, q, sems.at[0]) for q in range(2)]
     zcols = norms_of(p_ref)
-    leaving = []
     for q in range(2):
         finish(1, p_ref, qf_ref, num_ref, den_ref, win_ref, out_ref, q, zcols)
-        leaving.append(leave(out_ref, out_hbm, 1 - core_ref[0], q, out_sems))
+        leaving.append(leave(out_ref, out_hbm, 1 - core, q, sems.at[1]))
     for copy in leaving:
         copy.wait()
 
@@ -322,14 +319,13 @@
     return pl.BlockSpec(memory_space=kind)
 
 
-def call(kernel, ins, outs, scratch, flops, moved, name, aliases={}):
+def call(kernel, ins, outs, scratch, flops, moved, name):
     made = pl.pallas_call(
         kernel,
         out_shape=[pltpu.HBM(o.shape, o.dtype) if k == HB else o for o, k in outs],
         in_specs=[spec(k) for k in ins],
         out_specs=[spec(k) for _, k in outs],
         scratch_shapes=scratch,
-        input_output_aliases=aliases,
         compiler_params=pltpu.CompilerParams(vmem_limit_bytes=40 * 2**20),
         cost_estimate=pl.CostEstimate(flops=flops, bytes_accessed=moved, transcendentals=0),
         name=name,
@@ -392,19 +388,25 @@
 OUT_SCRATCH = [pltpu.VMEM(HALF, BF16), pltpu.SemaphoreType.DMA((2,))]
 
 
-def final_first(core, prior, qf, num, den, win):
-    return call(
-        first_kernel, [SM, VM] + [HB] * 4,
-        [OUT, (shape(*HALF_QF, dtype=BF16), VM), (shape(*HALF), VM), (shape(*DENS), VM), (shape(*HALF), VM)],
-        [pltpu.VMEM(HALF_QF, BF16), pltpu.VMEM(HALF, F32), pltpu.VMEM(HALF, F32), OUT_SCRATCH[0],
-         pltpu.SemaphoreType.DMA((3, 4)), OUT_SCRATCH[1]],
-        2 * 10**9, 10**7, "first",
-    )(core, prior, qf, num, den, win)
+def stage(core, qf, num, den, win):
+    half = [(shape(*HALF_QF, dtype=BF16), VM), (shape(*HALF), VM)]
+    return call(
+        stage_kernel, [SM] + [HB] * 4, half + [(shape(*HALF), VM)] + half + [(shape(*DENS), VM)],
+        [pltpu.SemaphoreType.DMA((8,))], 10**9, 10**7, "stage",
+    )(core, qf, num, den, win)
+
+
+def final_first(core, prior, qf, num, den, own_win, win):
+    return call(
+        first_kernel, [SM] + [VM] * 5 + [HB], [(shape(*HALF, dtype=BF16), VM), (shape(*HALF), VM)],
+        [pltpu.SemaphoreType.DMA((1,))], 2 * 10**9, 10**6, "first",
+    )(core, prior, qf, num, den, own_win, win)
 
 
 def final_second(core, prior, qf, num, den, win, done):
     return call(
-        second_kernel, [SM] + [VM] * 5 + [HB], [OUT], OUT_SCRATCH, 2 * 10**9, 10**6, "second", {6: 0}
+        second_kernel, [SM] + [VM] * 6, [(shape(ROWS, VALUES, dtype=BF16), HB)],
+        [pltpu.VMEM(HALF, BF16), pltpu.SemaphoreType.DMA((2, 2))], 2 * 10**9, 10**6, "second",
     )(core, prior, qf, num, den, win, done)[0]
 
 
@@ -449,11 +451,13 @@
     back, wq = after(back.reshape(PIECES, *PIECE), wq)
     mine = exchange(back, ("x", "z"))
     win = window(start, wq, wk, v, hk, hv)
-    mine, win = after(mine, win)
+    staged = stage(core, qf, num, den, win)
+    mine, *staged = after(mine, *staged)
+    qf0, num0, win0, qf1, num1, den = staged
     mine = mine.reshape(half, PAIR_ROWS, LANES)
     other = swap(mine)
-    done, *rest = final_first(core, mine, qf, num, den, win)
-    return final_second(core, other, *rest, done)
+    done, win1 = final_first(core, mine, qf0, num0, den, win0, win)
+    return final_second(core, other, qf1, num1, den, win1, done)
 
 
 def solution(mesh):

time: 76.5 us -> 74.7 us (0.976)
  waiting for transfers between devices: 14.2 us -> 12.5 us
    all_to_all x3, waiting for transfers between devices: 12.5 us -> 10.6 us  [exchange(): return lax.all_to_all(array, axes, split_axis=0, concat_axis=0, tiled=True)]
    pallas_call x7 -> x8, Pallas kernels: 16.8 us -> 16.6 us  [call(): made(*(pltpu.with_memory_space_constraint(a, k) if k == HB else a for a,...]
  transfers between devices with their start and end apart: 7 -> 7, of which waited for: 4 -> 5; matrix products, arithmetic and copies ran while one was open for 1% -> 1% of each run, Pallas kernels for 17% -> 18%
where the time goes in v3:
time: 74.7 us; the launch traced here: 74.1 us
  starting transfers between devices  43.3 us (58%)
  Pallas kernels  16.6 us (22%)
  waiting for transfers between devices  12.5 us (17%)
  other arithmetic  0.84 us (1%)
    all_to_all x3, starting transfers between devices, exchange(): return lax.all_to_all(array, axes, split_axis=0, concat_axis=0, tiled=True)  22.2 us
    pallas_call x8, Pallas kernels, call(): made(*(pltpu.with_memory_space_constraint(a, k) if k == HB else a for a,...  16.6 us
    ppermute x2, starting transfers between devices, swap(): return lax.ppermute(array, 'c', [(0, 1), (1, 0)])  15.2 us
    all_to_all x3, waiting for transfers between devices, exchange(): return lax.all_to_all(array, axes, split_axis=0, concat_axis=0, tiled=True)  10.6 us
    ppermute x1, starting transfers between devices, body(): hk = lax.ppermute(wk_out, AXES, pairs)  3.96 us
    ppermute x1, starting transfers between devices, body(): hv = lax.ppermute(v_out, AXES, pairs)  1.92 us
    ppermute x2, waiting for transfers between devices, swap(): return lax.ppermute(array, 'c', [(0, 1), (1, 0)])  1.87 us
  transfers between devices with their start and end apart: 7, of which 5 were waited for; matrix products, arithmetic and copies ran while one was open for 1% of the time, Pallas kernels for 18%

profile of v3, /device:TPU:1, one launch (start us, length us, event | category | flops | bytes accessed | tf_op | source)
XLA Modules:
  0.0 74.1 jit_solution(2652914767979230696)
XLA Ops:
  0.0 1.8 %state.1 = f32[8,160,128]{2,1,0:T(8,128)S(1)} custom-call(s32[1]{0:T(128)} %bitcast.core_ref, bf16[256,256]{1,0:T(8,128)(2,1)} %fk_ref, bf16[256,1024]{1,0:T(8,128)(2,1)} %v_ref.3), custom_call_target="tpu_custom_call" | custom-call | flops 1000000000 | bytes 5000000 | tf_op jit(solution)/shard_map/state/pallas_call | solution.py:333
  1.9 0.0 copy-start
  1.9 0.0 copy-start.3
  1.9 0.0 copy-start.4
  1.9 8.9 %collective-permute-start = (f32[8,160,128]{2,1,0:T(8,128)S(1)}, f32[8,160,128]{2,1,0:T(8,128)S(1)}, u32[]{:S(2)}, u32[]{:S(2)}) collective-permute-start(f32[8,160,128]{2,1,0:T(8,128)S(1)} %state.1), channel_id=1, source_target_pairs={{0,1},{1,0},{2,3},{3,2},{4,5},{5,4},{6,7},{7,6},{8,9},{9,8},{10,11... | collective-permute-start | bytes 1966088 | tf_op jit(solution)/shard_map/ppermute | solution.py:418
  10.8 1.7 %collective-permute-done.sib_ref = f32[8,160,128]{2,1,0:T(8,128)S(1)} collective-permute-done((f32[8,160,128]{2,1,0:T(8,128)S(1)}, f32[8,160,128]{2,1,0:T(8,128)S(1)}, u32[]{:S(2)}, u32[]{:S(2)}) %collective-permute-start) | collective-permute-done | bytes 655392 | tf_op jit(solution)/shard_map/ppermute | solution.py:418
  12.5 0.8 %slice_add_fusion = f32[4,160,128]{2,1,0:T(8,128)} fusion(f32[8,160,128]{2,1,0:T(8,128)S(1)} %collective-permute-done.sib_ref, f32[8,160,128]{2,1,0:T(8,128)S(1)} %state.1), kind=kLoop, calls=%fused_computation | loop fusion | flops 81920 | bytes 983040 | tf_op jit(solution)/shard_map/add | solution.py:435
  13.3 7.5 %all-to-all-start = ((f32[32,5,4,128]{3,2,1,0:T(4,128)}), f32[32,5,4,128]{3,2,1,0:T(4,128)S(1)}, u32[]{:S(2)}, u32[]{:S(2)}) async-start(f32[32,5,4,128]{3,2,1,0:T(4,128)} %bitcast.2), calls=%async_computation | async-start | bytes 655360 | tf_op jit(solution)/shard_map/all_to_all | solution.py:414
  20.8 0.0 copy-done
  20.8 0.0 copy-done.3
  20.8 0.0 copy-done.4
  20.9 0.0 copy-start.2
  20.9 4.1 %intra.1 = (bf16[20,256,128]{2,1,0:T(8,128)(2,1)}, f32[4,256,256]{2,1,0:T(8,128)}, f32[256,128]{1,0:T(8,128)}) custom-call(s32[1]{0:T(128)} %bitcast.core_ref, bf16[256,256]{1,0:T(8,128)(2,1)S(1)} %copy-done.4, bf16[256,256]{1,0:T(8,128)(2,1)S(1)} %copy-done.3, bf16[256,1024]{1,0:T(8,128)(2,1)S(1)} %copy-done, f32[8,160,128]{2,1,0:T(8,128)S(1)} %collective-permute-done.sib_ref), custom_call_target="tpu_custom_call" | custom-call | flops 2000000000 | bytes 16000000 | tf_op jit(solution)/shard_map/intra/pallas_call | solution.py:333
  25.0 0.0 copy-done.2
  25.0 4.0 %collective-permute-start.1 = (bf16[256,1024]{1,0:T(8,128)(2,1)S(1)}, bf16[256,1024]{1,0:T(8,128)(2,1)S(1)}, u32[]{:S(2)}, u32[]{:S(2)}) collective-permute-start(bf16[256,1024]{1,0:T(8,128)(2,1)S(1)} %copy-done.2), channel_id=1, source_target_pairs={{0,1},{1,2},{2,3},{3,4},{4,5},{5,6},{6,7},{7,8},{8,9},{9,10},{10,1... | collective-permute-start | bytes 1572872 | tf_op jit(solution)/shard_map/ppermute | solution.py:442
  29.0 1.9 %collective-permute-start.2 = (bf16[256,1024]{1,0:T(8,128)(2,1)S(1)}, bf16[256,1024]{1,0:T(8,128)(2,1)}, u32[]{:S(2)}, u32[]{:S(2)}) collective-permute-start(bf16[256,1024]{1,0:T(8,128)(2,1)S(1)} %copy-done), channel_id=1, source_target_pairs={{0,1},{1,2},{2,3},{3,4},{4,5},{5,6},{6,7},{7,8},{8,9},{9,10},{10,1... | collective-permute-start | bytes 1572872 | tf_op jit(solution)/shard_map/ppermute | solution.py:443
  30.9 0.4 all-to-all-done
  31.3 0.1 reduce_sum.9
  31.4 0.6 broadcast_in_dim.3
  32.0 6.8 %all-to-all-start.1 = ((f32[8,5,4,128]{3,2,1,0:T(4,128)}), f32[8,5,4,128]{3,2,1,0:T(4,128)S(1)}, u32[]{:S(2)}, u32[]{:S(2)}) async-start(f32[8,5,4,128]{3,2,1,0:T(4,128)} %broadcast_in_dim.3), calls=%async_computation.1 | async-start | bytes 163840 | tf_op jit(solution)/shard_map/all_to_all | solution.py:414
  38.9 0.0 copy-start.1
  38.9 7.4 %all-to-all-done.1 = f32[8,5,4,128]{3,2,1,0:T(4,128)S(1)} async-done(((f32[8,5,4,128]{3,2,1,0:T(4,128)}), f32[8,5,4,128]{3,2,1,0:T(4,128)S(1)}, u32[]{:S(2)}, u32[]{:S(2)}) %all-to-all-start.1) | async-done | bytes 81952 | tf_op jit(solution)/shard_map/all_to_all | solution.py:414
  46.2 0.8 %spread.1 = f32[640,128]{1,0:T(8,128)} custom-call(s32[1]{0:T(128)} %bitcast.1.y_ref, f32[640,128]{1,0:T(8,128)S(1)} %inner.1.inner_ref, f32[160,128]{1,0:T(8,128)S(1)} %bitcast.9), custom_call_target="tpu_custom_call" | custom-call | flops 1000000 | bytes 1000000 | tf_op jit(solution)/shard_map/spread/pallas_call | solution.py:333
  47.0 7.9 %all-to-all-start.2 = ((f32[32,5,4,128]{3,2,1,0:T(4,128)}), f32[32,5,4,128]{3,2,1,0:T(4,128)S(1)}, u32[]{:S(2)}, u32[]{:S(2)}) async-start(f32[32,5,4,128]{3,2,1,0:T(4,128)} %bitcast.5), calls=%async_computation.2 | async-start | bytes 655360 | tf_op jit(solution)/shard_map/all_to_all | solution.py:414
  54.9 0.0 collective-permute-done.1.hk_ref
  54.9 0.0 collective-permute-done.2.hv_ref
  54.9 0.0 copy-done.1
  54.9 5.2 %window.1.win_hbm = f32[4,256,256]{2,1,0:T(8,128)} custom-call(s32[1]{0:T(128)} %bitcast.6.start_ref, bf16[256,1024]{1,0:T(8,128)(2,1)S(1)} %copy-done.1, bf16[256,1024]{1,0:T(8,128)(2,1)S(1)} %copy-done.2, bf16[256,1024]{1,0:T(8,128)(2,1)S(1)} %copy-done, bf16[256,1024]{1,0:T(8,128)(2,1)S(1)} %collective-permute-done.1.hk_ref, ...), custom_call_target="tpu_custom_call" | custom-call | flops 2000000000 | bytes 16000000 | tf_op jit(solution)/shard_map/window/pallas_call | solution.py:333
  60.1 1.9 %stage.1 = (bf16[10,256,128]{2,1,0:T(8,128)(2,1)S(1)}, f32[2,256,256]{2,1,0:T(8,128)S(1)}, f32[2,256,256]{2,1,0:T(8,128)S(1)}, bf16[10,256,128]{2,1,0:T(8,128)(2...) custom-call(s32[1]{0:T(128)} %bitcast.core_ref, bf16[20,256,128]{2,1,0:T(8,128)(2,1)} %get-tuple-element.52.qf_hbm, ...), custom_call_target="tpu_custom_call" | custom-call | flops 1000000000 | bytes 10000000 | tf_op jit(solution)/shard_map/stage/pallas_call | solution.py:333
  62.0 2.8 %all-to-all-done.2 = f32[32,5,4,128]{3,2,1,0:T(4,128)S(1)} async-done(((f32[32,5,4,128]{3,2,1,0:T(4,128)}), f32[32,5,4,128]{3,2,1,0:T(4,128)S(1)}, u32[]{:S(2)}, u32[]{:S(2)}) %all-to-all-start.2) | async-done | bytes 327712 | tf_op jit(solution)/shard_map/all_to_all | solution.py:414
  64.8 6.3 %collective-permute-start.3 = (f32[4,160,128]{2,1,0:T(8,128)S(1)}, f32[4,160,128]{2,1,0:T(8,128)S(1)}, u32[]{:S(2)}, u32[]{:S(2)}) collective-permute-start(f32[4,160,128]{2,1,0:T(8,128)S(1)} %bitcast.10), channel_id=1, source_target_pairs={{0,1},{1,0},{2,3},{3,2},{4,5},{5,4},{6,7},{7,6},{8,9},{9,8},{10,11... | collective-permute-start | bytes 983048 | tf_op jit(solution)/shard_map/ppermute | solution.py:418
  71.1 1.1 %first.1 = (bf16[2,256,256]{2,1,0:T(8,128)(2,1)S(1)}, f32[2,256,256]{2,1,0:T(8,128)S(1)}) custom-call(s32[1]{0:T(128)} %bitcast.core_ref, f32[4,160,128]{2,1,0:T(8,128)S(1)} %bitcast.11, bf16[10,256,128]{2,1,0:T(8,128)(2,1)S(1)} %get-tuple-element.68.qf_ref, f32[2,256,256]{2,1,0:T(8,128)S(1)} %get-tuple-element.69.num_ref, ...), custom_call_target="tpu_custom_call" | custom-call | flops 2000000000 | bytes 1000000 | tf_op jit(solution)/shard_map/first/pallas_call | solution.py:333
  72.2 0.2 collective-permute-done.3.p_ref
  72.4 1.7 %second.1 = bf16[256,1024]{1,0:T(8,128)(2,1)} custom-call(s32[1]{0:T(128)} %bitcast.core_ref, f32[4,160,128]{2,1,0:T(8,128)S(1)} %collective-permute-done.3.p_ref, bf16[10,256,128]{2,1,0:T(8,128)(2,1)S(1)} %get-tuple-element.65.qf_ref, f32[2,256,256]{2,1,0:T(8,128)S(1)} %get-tuple-element.66.num_ref, f32[256,128]{1,0:T(8,128)S(1)} %get-tuple-element.67.den_ref, ...), custom_call_target="tpu_custom_call" | custom-call | flops 2000000000 | bytes 1000000 | tf_op jit(solution)/shard_map/second/pallas_call | solution.py:333
  (1 shorter events, 0.0 us)
Async XLA Ops:
  1.9 19.0 %copy-start = (bf16[256,1024]{1,0:T(8,128)(2,1)S(1)}, bf16[256,1024]{1,0:T(8,128)(2,1)}, u32[]{:S(2)}) copy-start(bf16[256,1024]{1,0:T(8,128)(2,1)} %v_ref.3) | copy-start | bytes 1572868
  1.9 19.0 %copy-start.3 = (bf16[256,256]{1,0:T(8,128)(2,1)S(1)}, bf16[256,256]{1,0:T(8,128)(2,1)}, u32[]{:S(2)}) copy-start(bf16[256,256]{1,0:T(8,128)(2,1)} %fk_ref) | copy-start | bytes 393220
  1.9 19.0 %copy-start.4 = (bf16[256,256]{1,0:T(8,128)(2,1)S(1)}, bf16[256,256]{1,0:T(8,128)(2,1)}, u32[]{:S(2)}) copy-start(bf16[256,256]{1,0:T(8,128)(2,1)} %fq_ref) | copy-start | bytes 393220
  1.9 10.6 %collective-permute-start = (f32[8,160,128]{2,1,0:T(8,128)S(1)}, f32[8,160,128]{2,1,0:T(8,128)S(1)}, u32[]{:S(2)}, u32[]{:S(2)}) collective-permute-start(f32[8,160,128]{2,1,0:T(8,128)S(1)} %state.1), channel_id=1, source_target_pairs={{0,1},{1,0},{2,3},{3,2},{4,5},{5,4},{6,7},{7,6},{8,9},{9,8},{10,11... | collective-permute-start | bytes 1966088 | tf_op jit(solution)/shard_map/ppermute | solution.py:418
  13.3 18.0 %all-to-all-start = ((f32[32,5,4,128]{3,2,1,0:T(4,128)}), f32[32,5,4,128]{3,2,1,0:T(4,128)S(1)}, u32[]{:S(2)}, u32[]{:S(2)}) async-start(f32[32,5,4,128]{3,2,1,0:T(4,128)} %bitcast.2), calls=%async_computation | async-start | bytes 655360 | tf_op jit(solution)/shard_map/all_to_all | solution.py:414
  20.9 4.1 %copy-start.2 = (bf16[256,1024]{1,0:T(8,128)(2,1)S(1)}, bf16[256,1024]{1,0:T(8,128)(2,1)}, u32[]{:S(2)}) copy-start(bf16[256,1024]{1,0:T(8,128)(2,1)} %k_ref.1) | copy-start | bytes 1572868
  25.0 29.9 %collective-permute-start.1 = (bf16[256,1024]{1,0:T(8,128)(2,1)S(1)}, bf16[256,1024]{1,0:T(8,128)(2,1)S(1)}, u32[]{:S(2)}, u32[]{:S(2)}) collective-permute-start(bf16[256,1024]{1,0:T(8,128)(2,1)S(1)} %copy-done.2), channel_id=1, source_target_pairs={{0,1},{1,2},{2,3},{3,4},{4,5},{5,6},{6,7},{7,8},{8,9},{9,10},{10,1... | collective-permute-start | bytes 1572872 | tf_op jit(solution)/shard_map/ppermute | solution.py:442
  29.0 26.0 %collective-permute-start.2 = (bf16[256,1024]{1,0:T(8,128)(2,1)S(1)}, bf16[256,1024]{1,0:T(8,128)(2,1)}, u32[]{:S(2)}, u32[]{:S(2)}) collective-permute-start(bf16[256,1024]{1,0:T(8,128)(2,1)S(1)} %copy-done), channel_id=1, source_target_pairs={{0,1},{1,2},{2,3},{3,4},{4,5},{5,6},{6,7},{7,8},{8,9},{9,10},{10,1... | collective-permute-start | bytes 1572872 | tf_op jit(solution)/shard_map/ppermute | solution.py:443
  32.0 14.2 %all-to-all-start.1 = ((f32[8,5,4,128]{3,2,1,0:T(4,128)}), f32[8,5,4,128]{3,2,1,0:T(4,128)S(1)}, u32[]{:S(2)}, u32[]{:S(2)}) async-start(f32[8,5,4,128]{3,2,1,0:T(4,128)} %broadcast_in_dim.3), calls=%async_computation.1 | async-start | bytes 163840 | tf_op jit(solution)/shard_map/all_to_all | solution.py:414
  38.9 16.1 %copy-start.1 = (bf16[256,1024]{1,0:T(8,128)(2,1)S(1)}, bf16[256,1024]{1,0:T(8,128)(2,1)}, u32[]{:S(2)}) copy-start(bf16[256,1024]{1,0:T(8,128)(2,1)} %q_ref) | copy-start | bytes 1572868
  47.0 17.9 %all-to-all-start.2 = ((f32[32,5,4,128]{3,2,1,0:T(4,128)}), f32[32,5,4,128]{3,2,1,0:T(4,128)S(1)}, u32[]{:S(2)}, u32[]{:S(2)}) async-start(f32[32,5,4,128]{3,2,1,0:T(4,128)} %bitcast.5), calls=%async_computation.2 | async-start | bytes 655360 | tf_op jit(solution)/shard_map/all_to_all | solution.py:414
  64.8 7.5 %collective-permute-start.3 = (f32[4,160,128]{2,1,0:T(8,128)S(1)}, f32[4,160,128]{2,1,0:T(8,128)S(1)}, u32[]{:S(2)}, u32[]{:S(2)}) collective-permute-start(f32[4,160,128]{2,1,0:T(8,128)S(1)} %bitcast.10), channel_id=1, source_target_pairs={{0,1},{1,0},{2,3},{3,2},{4,5},{5,4},{6,7},{7,6},{8,9},{9,8},{10,11... | collective-permute-start | bytes 983048 | tf_op jit(solution)/shard_map/ppermute | solution.py:418

commit v4 on v3

--- a/solution.py
+++ b/solution.py
@@ -48,25 +48,14 @@
     return lax.broadcasted_iota(jnp.int32, (rows, LANES), 1) < 64
 
 
-def state_kernel(core_ref, fk_hbm, v_hbm, out_ref, fk_ref, v_ref, kt_ref, sems):
-    half = VALUES // 2
-    copies = [pltpu.make_async_copy(fk_hbm, fk_ref, sems.at[0])]
-    for i in range(2):
-        lanes = pl.ds(i * half, half)
-        copies.append(pltpu.make_async_copy(v_hbm.at[:, lanes], v_ref.at[:, lanes], sems.at[1 + i]))
-    for copy in copies:
-        copy.start()
-    first = core_ref[0] * (PAIRS // 2)
-    copies[0].wait()
-    kt_ref[...] = fk_ref[...].astype(F32).T
+def half_state(first, kt_ref, v_ref):
     lane = lax.broadcasted_iota(jnp.int32, (FROWS, LANES), 1)
     low = lane < 64
     vlow = low_lanes(ROWS)
     zcols = jnp.zeros((FROWS, LANES), F32)
-    copies[1].wait()
-    copies[2].wait()
-    for i in range(PAIRS):
-        pair = lax.rem(first + i, PAIRS)
+    states = []
+    for i in range(PAIRS // 2):
+        pair = first + i
         x = kt_ref[pl.ds(pl.multiple_of(pair * 32, 32), 32), :]
         v = v_ref[:, pl.ds(pl.multiple_of(pair * LANES, LANES), LANES)]
         one = jnp.ones_like(v)
@@ -74,19 +63,40 @@
         fb = features(x[DIM:]).astype(BF16)
         sa = jnp.dot(fa, jnp.where(vlow, v, one), preferred_element_type=F32)
         sb = jnp.dot(fb, jnp.where(vlow, one, v), preferred_element_type=F32)
-        out_ref[i, :FROWS] = jnp.where(low, sa, sb)
+        states.append(jnp.where(low, sa, sb))
         z = jnp.where(low, sb, sa)
         zcols = jnp.where((lane == i) | (lane == 64 + i), z, zcols)
     zrows = zcols.T
     blank = jnp.zeros((8, 2 * LANES - FROWS), F32)
     row = lax.broadcasted_iota(jnp.int32, (8, LANES), 0)
-    for i in range(PAIRS):
-        tail = out_ref[i, TAIL]
+    for i in range(PAIRS // 2):
+        tail = states[i][TAIL]
         for at, src in ((1, 64 + i), (3, i)):
             z = jnp.concatenate([jnp.broadcast_to(zrows[src : src + 1], (8, FROWS)), blank], 1)
             tail = jnp.where(row == at, z[:, :LANES], tail)
             tail = jnp.where(row == at + 1, z[:, LANES:], tail)
-        out_ref[i, TAIL] = tail
+        states[i] = jnp.concatenate([states[i][: TAIL.start], tail], 0)
+    return states
+
+
+def other_kernel(core_ref, fk_hbm, v_hbm, out_ref, kt_ref, v_ref, fk_ref, sems):
+    copies = [
+        pltpu.make_async_copy(fk_hbm, fk_ref, sems.at[0]),
+        pltpu.make_async_copy(v_hbm, v_ref, sems.at[1]),
+    ]
+    for copy in copies:
+        copy.start()
+    copies[0].wait()
+    kt_ref[...] = fk_ref[...].astype(F32).T
+    copies[1].wait()
+    for i, state in enumerate(half_state((1 - core_ref[0]) * (PAIRS // 2), kt_ref, v_ref)):
+        out_ref[i] = state
+
+
+def chip_kernel(core_ref, kt_ref, v_ref, got_ref, mine_ref, chip_ref):
+    for i, state in enumerate(half_state(core_ref[0] * (PAIRS // 2), kt_ref, v_ref)):
+        mine_ref[i] = state
+        chip_ref[i] = state + got_ref[i]
 
 
 def inner_kernel(p_ref, out_ref):
@@ -143,7 +153,7 @@
     return jnp.where(tlow, res[0], res[1]), jnp.where(tlow, res[1], res[0])
 
 
-def intra_kernel(core_ref, fq_ref, fk_ref, v_ref, sib_ref, qf_hbm, num_hbm, den_hbm, qt_ref, kt_ref, qf_ref, num_ref, den_ref, sems):
+def intra_kernel(core_ref, fq_ref, fk_ref, v_ref, low_ref, high_ref, qf_hbm, num_hbm, den_hbm, qt_ref, kt_ref, qf_ref, num_ref, den_ref, sems):
     second = core_ref[0] == 1
     qt_ref[...] = fq_ref[...].astype(F32).T
     kt_ref[...] = fk_ref[...].astype(F32).T
@@ -152,7 +162,8 @@
     causal = lax.broadcasted_iota(jnp.int32, (ROWS, ROWS), 0) >= lax.broadcasted_iota(
         jnp.int32, (ROWS, ROWS), 1
     )
-    zcols = norm_columns([sib_ref[i, TAIL] for i in range(PAIRS)])
+    sibs = [(low_ref, high_ref)[i // 4].at[i % 4] for i in range(PAIRS)]
+    zcols = norm_columns([sib[TAIL] for sib in sibs])
     zcols = jnp.where(second, zcols, F32(0.0))
     all_dens = jnp.zeros((ROWS, LANES), F32)
     copies = []
@@ -184,7 +195,7 @@
         nums = jnp.dot(jnp.concatenate(rounded, 0), v_ref[:, wide], preferred_element_type=F32)
         for p in range(2):
             pair = 2 * quad + p
-            s = jnp.where(second, sib_ref[pair], F32(0.0))
+            s = jnp.where(second, sibs[pair][...], F32(0.0))
             num, den = cross(qfs[2 * p : 2 * p + 2], s, zcols, 2 * pair, 2 * p)
             here = slice(p * LANES, (p + 1) * LANES)
             n0 = nums[2 * p * ROWS : (2 * p + 1) * ROWS, here]
@@ -349,12 +360,21 @@
 HALF = (2, ROWS, 256)
 
 
-def own_state(core, fk, v):
-    return call(
-        state_kernel, [SM, HB, HB], [(shape(PAIRS, PAIR_ROWS, LANES), VM)],
-        [pltpu.VMEM((ROWS, 256), BF16), pltpu.VMEM((ROWS, VALUES), BF16), TURNED, pltpu.SemaphoreType.DMA((3,))],
-        10**9, 5 * 10**6, "state",
-    )(core, fk, v)[0]
+STATES = (PAIRS // 2, PAIR_ROWS, LANES)
+
+
+def other_state(core, fk, v):
+    return call(
+        other_kernel, [SM, HB, HB],
+        [(shape(*STATES), VM), (shape(256, ROWS), VM), (shape(ROWS, VALUES, dtype=BF16), VM)],
+        [pltpu.VMEM((ROWS, 256), BF16), pltpu.SemaphoreType.DMA((2,))], 10**9, 5 * 10**6, "other",
+    )(core, fk, v)
+
+
+def chip_state(core, kt, v, got):
+    return call(
+        chip_kernel, [SM, VM, VM, VM], [(shape(*STATES), VM), (shape(*STATES), VM)], [], 10**9, 10**6, "chip"
+    )(core, kt, v, got)
 
 
 def inner(pieces):
@@ -368,13 +388,13 @@
     )[0]
 
 
-def intra(core, fq, fk, v, sib):
-    return call(
-        intra_kernel, [SM, VM, VM, VM, VM],
+def intra(core, fq, fk, v, low, high):
+    return call(
+        intra_kernel, [SM] + [VM] * 5,
         [(shape(*QF, dtype=BF16), HB), (shape(*BY_QUADS), HB), (shape(*DENS), HB)],
         [TURNED, TURNED, pltpu.VMEM(QF, BF16), WIDE, pltpu.VMEM(DENS, F32), pltpu.SemaphoreType.DMA((4, 4))],
         2 * 10**9, 16 * 10**6, "intra",
-    )(core, fq, fk, v, sib)
+    )(core, fq, fk, v, low, high)
 
 
 def window(start, q, k, v, hk, hv):
@@ -429,24 +449,24 @@
 def body(fq, fk, v, wq, wk):
     core = scalar(lax.axis_index("c"))
     start = scalar(lax.axis_index(AXES))
-    state = own_state(core, fk, v)
-    sib = swap(state)
     half = PAIRS // 2
-    chip = (state[:half] + sib[half:]).reshape(PIECES, *PIECE)
-    chip, fq, fk = after(chip, fq, fk)
+    state, turned, held = other_state(core, fk, v)
+    got = swap(state)
+    own, chip = chip_state(core, turned, held, got)
+    chip, own = after(chip.reshape(PIECES, *PIECE), own)
     pieces = exchange(chip, ("x", "z"))
-    qf, num, den = intra(core, fq, fk, v, sib)
+    low, wk_out, v_out = after(swap(own), wk, v)
     count = lax.axis_size(AXES)
     pairs = [(i, i + 1) for i in range(count - 1)]
-    qf, wk_out, v_out = after(qf, wk, v)
     hk = lax.ppermute(wk_out, AXES, pairs)
     hv = lax.ppermute(v_out, AXES, pairs)
-    pieces, qf, num, den = after(pieces, qf, num, den)
+    pieces, low = after(pieces, low)
     total = jnp.broadcast_to(jnp.sum(pieces, 0), (8, *PIECE))
-    total, pieces = after(total, pieces)
+    total, pieces, low, fq, fk = after(total, pieces, low, fq, fk)
     rows = exchange(total, "y")
     before = inner(pieces)
-    rows, before = after(rows, before)
+    qf, num, den = intra(core, fq, fk, v, low, got)
+    rows, before, qf, num, den = after(rows, before, qf, num, den)
     back = spread(scalar(lax.axis_index("y")), before, rows)
     back, wq = after(back.reshape(PIECES, *PIECE), wq)
     mine = exchange(back, ("x", "z"))

time: 74.7 us -> 74.2 us (level)
  waiting for transfers between devices: 12.5 us -> 9.71 us
  starting transfers between devices: 43.3 us -> 45.6 us
  local copies, waits for them, and re-layouts: 0.68 us -> 1.64 us
  other arithmetic: 0.84 us -> 0.07 us
    all_to_all x3, waiting for transfers between devices: 10.6 us -> 7.07 us  [exchange(): return lax.all_to_all(array, axes, split_axis=0, concat_axis=0, tiled=True)]
    ppermute x2 -> x3, starting transfers between devices: 15.2 us -> 17.8 us  [swap(): return lax.ppermute(array, 'c', [(0, 1), (1, 0)])]
    unnamed x10 -> x14, local copies, waits for them, and re-layouts: 0.03 us -> 0.99 us
    add x1 -> x0, other arithmetic: 0.77 us -> none  [body(): chip = (state[:half] + sib[half:]).reshape(PIECES, *PIECE)]
    ppermute x2 -> x3, waiting for transfers between devices: 1.87 us -> 2.63 us  [swap(): return lax.ppermute(array, 'c', [(0, 1), (1, 0)])]
    pallas_call x8 -> x9, Pallas kernels: 16.6 us -> 16.4 us  [call(): made(*(pltpu.with_memory_space_constraint(a, k) if k == HB else a for a,...]
  transfers between devices with their start and end apart: 7 -> 8, of which waited for: 5 -> 6; matrix products, arithmetic and copies ran while one was open for 1% -> 1% of each run, Pallas kernels for 18% -> 16%
where the time goes in v4:
time: 74.2 us; the launch traced here: 73.6 us
  starting transfers between devices  45.6 us (61%)
  Pallas kernels  16.4 us (22%)
  waiting for transfers between devices  9.71 us (13%)
  local copies, waits for them, and re-layouts  1.64 us (2%)
    all_to_all x3, starting transfers between devices, exchange(): return lax.all_to_all(array, axes, split_axis=0, concat_axis=0, tiled=True)  22.1 us
    ppermute x3, starting transfers between devices, swap(): return lax.ppermute(array, 'c', [(0, 1), (1, 0)])  17.8 us
    pallas_call x9, Pallas kernels, call(): made(*(pltpu.with_memory_space_constraint(a, k) if k == HB else a for a,...  16.4 us
    all_to_all x3, waiting for transfers between devices, exchange(): return lax.all_to_all(array, axes, split_axis=0, concat_axis=0, tiled=True)  7.07 us
    ppermute x1, starting transfers between devices, body(): hk = lax.ppermute(wk_out, AXES, pairs)  3.67 us
    ppermute x3, waiting for transfers between devices, swap(): return lax.ppermute(array, 'c', [(0, 1), (1, 0)])  2.63 us
    ppermute x1, starting transfers between devices, body(): hv = lax.ppermute(v_out, AXES, pairs)  2.04 us
  transfers between devices with their start and end apart: 8, of which 6 were waited for; matrix products, arithmetic and copies ran while one was open for 1% of the time, Pallas kernels for 16%

profile of v4, /device:TPU:1, one launch (start us, length us, event | category | flops | bytes accessed | tf_op | source)
XLA Modules:
  0.0 73.6 jit_solution(519468178142385179)
XLA Ops:
  0.0 1.6 %other.1 = (f32[4,160,128]{2,1,0:T(8,128)S(1)}, f32[256,256]{1,0:T(8,128)S(1)}, bf16[256,1024]{1,0:T(8,128)(2,1)S(1)}) custom-call(s32[1]{0:T(128)} %bitcast.core_ref, bf16[256,256]{1,0:T(8,128)(2,1)} %fk_ref, bf16[256,1024]{1,0:T(8,128)(2,1)} %v_ref.3), custom_call_target="tpu_custom_call" | custom-call | flops 1000000000 | bytes 5000000 | tf_op jit(solution)/shard_map/other/pallas_call | solution.py:344
  1.6 8.8 %collective-permute-start = (f32[4,160,128]{2,1,0:T(8,128)S(1)}, f32[4,160,128]{2,1,0:T(8,128)S(1)}, u32[]{:S(2)}, u32[]{:S(2)}) collective-permute-start(f32[4,160,128]{2,1,0:T(8,128)S(1)} %get-tuple-element.49), channel_id=1, source_target_pairs={{0,1},{1,0},{2,3},{3,2},{4,5},{5,4},{6,7},{7,6},{8,9},{9,8},{10,11... | collective-permute-start | bytes 983048 | tf_op jit(solution)/shard_map/ppermute | solution.py:438
  10.4 1.2 %collective-permute-done.got_ref.high_ref = f32[4,160,128]{2,1,0:T(8,128)S(1)} collective-permute-done((f32[4,160,128]{2,1,0:T(8,128)S(1)}, f32[4,160,128]{2,1,0:T(8,128)S(1)}, u32[]{:S(2)}, u32[]{:S(2)}) %collective-permute-start) | collective-permute-done | bytes 327712 | tf_op jit(solution)/shard_map/ppermute | solution.py:438
  11.6 0.0 copy-start.2
  11.6 0.0 copy-start
  11.6 1.2 %chip.1 = (f32[4,160,128]{2,1,0:T(8,128)S(1)}, f32[4,160,128]{2,1,0:T(8,128)}) custom-call(s32[1]{0:T(128)} %bitcast.core_ref, f32[256,256]{1,0:T(8,128)S(1)} %get-tuple-element.47.kt_ref, bf16[256,1024]{1,0:T(8,128)(2,1)S(1)} %get-tuple-element.48.v_ref, f32[4,160,128]{2,1,0:T(8,128)S(1)} %collective-permute-done.got_ref.high_ref), custom_call_target="tpu_custom_call" | custom-call | flops 1000000000 | bytes 1000000 | tf_op jit(solution)/shard_map/chip/pallas_call | solution.py:344
  12.8 7.5 %all-to-all-start = ((f32[32,5,4,128]{3,2,1,0:T(4,128)}), f32[32,5,4,128]{3,2,1,0:T(4,128)S(1)}, u32[]{:S(2)}, u32[]{:S(2)}) async-start(f32[32,5,4,128]{3,2,1,0:T(4,128)} %bitcast.2), calls=%async_computation | async-start | bytes 655360 | tf_op jit(solution)/shard_map/all_to_all | solution.py:434
  20.3 2.6 %collective-permute-start.1 = (f32[4,160,128]{2,1,0:T(8,128)S(1)}, f32[4,160,128]{2,1,0:T(8,128)S(1)}, u32[]{:S(2)}, u32[]{:S(2)}) collective-permute-start(f32[4,160,128]{2,1,0:T(8,128)S(1)} %get-tuple-element.53), channel_id=1, source_target_pairs={{0,1},{1,0},{2,3},{3,2},{4,5},{5,4},{6,7},{7,6},{8,9},{9,8},{10,11... | collective-permute-start | bytes 983048 | tf_op jit(solution)/shard_map/ppermute | solution.py:438
  22.9 1.2 %collective-permute-done.1.low_ref = f32[4,160,128]{2,1,0:T(8,128)S(1)} collective-permute-done((f32[4,160,128]{2,1,0:T(8,128)S(1)}, f32[4,160,128]{2,1,0:T(8,128)S(1)}, u32[]{:S(2)}, u32[]{:S(2)}) %collective-permute-start.1) | collective-permute-done | bytes 327712 | tf_op jit(solution)/shard_map/ppermute | solution.py:438
  24.1 0.0 copy-done.2
  24.1 0.0 copy-start.3
  24.1 3.7 %collective-permute-start.2 = (bf16[256,1024]{1,0:T(8,128)(2,1)S(1)}, bf16[256,1024]{1,0:T(8,128)(2,1)S(1)}, u32[]{:S(2)}, u32[]{:S(2)}) collective-permute-start(bf16[256,1024]{1,0:T(8,128)(2,1)S(1)} %copy-done.2), channel_id=1, source_target_pairs={{0,1},{1,2},{2,3},{3,4},{4,5},{5,6},{6,7},{7,8},{8,9},{9,10},{10,1... | collective-permute-start | bytes 1572872 | tf_op jit(solution)/shard_map/ppermute | solution.py:461
  27.8 0.0 copy-done
  27.8 2.0 %collective-permute-start.3 = (bf16[256,1024]{1,0:T(8,128)(2,1)S(1)}, bf16[256,1024]{1,0:T(8,128)(2,1)S(1)}, u32[]{:S(2)}, u32[]{:S(2)}) collective-permute-start(bf16[256,1024]{1,0:T(8,128)(2,1)S(1)} %copy-done), channel_id=1, source_target_pairs={{0,1},{1,2},{2,3},{3,4},{4,5},{5,6},{6,7},{7,8},{8,9},{9,10},{10,1... | collective-permute-start | bytes 1572872 | tf_op jit(solution)/shard_map/ppermute | solution.py:462
  29.8 0.9 %all-to-all-done = f32[32,5,4,128]{3,2,1,0:T(4,128)S(1)} async-done(((f32[32,5,4,128]{3,2,1,0:T(4,128)}), f32[32,5,4,128]{3,2,1,0:T(4,128)S(1)}, u32[]{:S(2)}, u32[]{:S(2)}) %all-to-all-start) | async-done | bytes 327712 | tf_op jit(solution)/shard_map/all_to_all | solution.py:434
  30.7 0.1 reduce_sum.9
  30.8 0.6 broadcast_in_dim.3
  31.5 0.0 copy-done.3
  31.5 0.0 copy-start.5
  31.5 0.0 copy-start.6
  31.5 7.0 %all-to-all-start.1 = ((f32[8,5,4,128]{3,2,1,0:T(4,128)}), f32[8,5,4,128]{3,2,1,0:T(4,128)S(1)}, u32[]{:S(2)}, u32[]{:S(2)}) async-start(f32[8,5,4,128]{3,2,1,0:T(4,128)} %broadcast_in_dim.3), calls=%async_computation.1 | async-start | bytes 163840 | tf_op jit(solution)/shard_map/all_to_all | solution.py:434
  38.5 0.0 copy-done.5
  38.5 0.0 copy-done.6
  38.5 0.0 copy-start.4
  38.5 1.0 %copy-done.4 = f32[4,160,128]{2,1,0:T(8,128)S(1)} copy-done((f32[4,160,128]{2,1,0:T(8,128)S(1)}, f32[4,160,128]{2,1,0:T(8,128)}, u32[]{:S(2)}) %copy-start.4) | copy-done | bytes 327704
  39.5 4.1 %intra.1 = (bf16[20,256,128]{2,1,0:T(8,128)(2,1)}, f32[4,256,256]{2,1,0:T(8,128)}, f32[256,128]{1,0:T(8,128)}) custom-call(s32[1]{0:T(128)} %bitcast.core_ref, bf16[256,256]{1,0:T(8,128)(2,1)S(1)} %copy-done.6, bf16[256,256]{1,0:T(8,128)(2,1)S(1)} %copy-done.5, bf16[256,1024]{1,0:T(8,128)(2,1)S(1)} %copy-done, f32[4,160,128]{2,1,0:T(8,128)S(1)} %copy-done.4, ...), custom_call_target="tpu_custom_call" | custom-call | flops 2000000000 | bytes 16000000 | tf_op jit(solution)/shard_map/intra/pallas_call | solution.py:344
  43.6 0.0 copy-start.1
  43.6 2.3 %all-to-all-done.1 = f32[8,5,4,128]{3,2,1,0:T(4,128)S(1)} async-done(((f32[8,5,4,128]{3,2,1,0:T(4,128)}), f32[8,5,4,128]{3,2,1,0:T(4,128)S(1)}, u32[]{:S(2)}, u32[]{:S(2)}) %all-to-all-start.1) | async-done | bytes 81952 | tf_op jit(solution)/shard_map/all_to_all | solution.py:434
  45.9 0.8 %spread.1 = f32[640,128]{1,0:T(8,128)} custom-call(s32[1]{0:T(128)} %bitcast.1.y_ref, f32[640,128]{1,0:T(8,128)S(1)} %inner.1.inner_ref, f32[160,128]{1,0:T(8,128)S(1)} %bitcast.9), custom_call_target="tpu_custom_call" | custom-call | flops 1000000 | bytes 1000000 | tf_op jit(solution)/shard_map/spread/pallas_call | solution.py:344
  46.6 7.6 %all-to-all-start.2 = ((f32[32,5,4,128]{3,2,1,0:T(4,128)}), f32[32,5,4,128]{3,2,1,0:T(4,128)S(1)}, u32[]{:S(2)}, u32[]{:S(2)}) async-start(f32[32,5,4,128]{3,2,1,0:T(4,128)} %bitcast.5), calls=%async_computation.2 | async-start | bytes 655360 | tf_op jit(solution)/shard_map/all_to_all | solution.py:434
  54.3 0.0 collective-permute-done.2.hk_ref
  54.3 0.0 collective-permute-done.3.hv_ref
  54.3 0.0 copy-done.1
  54.3 4.1 %window.1.win_hbm = f32[4,256,256]{2,1,0:T(8,128)} custom-call(s32[1]{0:T(128)} %bitcast.6.start_ref, bf16[256,1024]{1,0:T(8,128)(2,1)S(1)} %copy-done.1, bf16[256,1024]{1,0:T(8,128)(2,1)S(1)} %copy-done.2, bf16[256,1024]{1,0:T(8,128)(2,1)S(1)} %copy-done, bf16[256,1024]{1,0:T(8,128)(2,1)S(1)} %collective-permute-done.2.hk_ref, ...), custom_call_target="tpu_custom_call" | custom-call | flops 2000000000 | bytes 16000000 | tf_op jit(solution)/shard_map/window/pallas_call | solution.py:344
  58.4 1.9 %stage.1 = (bf16[10,256,128]{2,1,0:T(8,128)(2,1)S(1)}, f32[2,256,256]{2,1,0:T(8,128)S(1)}, f32[2,256,256]{2,1,0:T(8,128)S(1)}, bf16[10,256,128]{2,1,0:T(8,128)(2...) custom-call(s32[1]{0:T(128)} %bitcast.core_ref, bf16[20,256,128]{2,1,0:T(8,128)(2,1)} %get-tuple-element.68.qf_hbm, ...), custom_call_target="tpu_custom_call" | custom-call | flops 1000000000 | bytes 10000000 | tf_op jit(solution)/shard_map/stage/pallas_call | solution.py:344
  60.3 3.9 %all-to-all-done.2 = f32[32,5,4,128]{3,2,1,0:T(4,128)S(1)} async-done(((f32[32,5,4,128]{3,2,1,0:T(4,128)}), f32[32,5,4,128]{3,2,1,0:T(4,128)S(1)}, u32[]{:S(2)}, u32[]{:S(2)}) %all-to-all-start.2) | async-done | bytes 327712 | tf_op jit(solution)/shard_map/all_to_all | solution.py:434
  64.2 6.5 %collective-permute-start.4 = (f32[4,160,128]{2,1,0:T(8,128)S(1)}, f32[4,160,128]{2,1,0:T(8,128)S(1)}, u32[]{:S(2)}, u32[]{:S(2)}) collective-permute-start(f32[4,160,128]{2,1,0:T(8,128)S(1)} %bitcast.10), channel_id=1, source_target_pairs={{0,1},{1,0},{2,3},{3,2},{4,5},{5,4},{6,7},{7,6},{8,9},{9,8},{10,11... | collective-permute-start | bytes 983048 | tf_op jit(solution)/shard_map/ppermute | solution.py:438
  70.7 1.1 %first.1 = (bf16[2,256,256]{2,1,0:T(8,128)(2,1)S(1)}, f32[2,256,256]{2,1,0:T(8,128)S(1)}) custom-call(s32[1]{0:T(128)} %bitcast.core_ref, f32[4,160,128]{2,1,0:T(8,128)S(1)} %bitcast.11, bf16[10,256,128]{2,1,0:T(8,128)(2,1)S(1)} %get-tuple-element.84.qf_ref, f32[2,256,256]{2,1,0:T(8,128)S(1)} %get-tuple-element.85.num_ref, ...), custom_call_target="tpu_custom_call" | custom-call | flops 2000000000 | bytes 1000000 | tf_op jit(solution)/shard_map/first/pallas_call | solution.py:344
  71.7 0.2 collective-permute-done.4.p_ref
  71.9 1.7 %second.1 = bf16[256,1024]{1,0:T(8,128)(2,1)} custom-call(s32[1]{0:T(128)} %bitcast.core_ref, f32[4,160,128]{2,1,0:T(8,128)S(1)} %collective-permute-done.4.p_ref, bf16[10,256,128]{2,1,0:T(8,128)(2,1)S(1)} %get-tuple-element.81.qf_ref, f32[2,256,256]{2,1,0:T(8,128)S(1)} %get-tuple-element.82.num_ref, f32[256,128]{1,0:T(8,128)S(1)} %get-tuple-element.83.den_ref, ...), custom_call_target="tpu_custom_call" | custom-call | flops 2000000000 | bytes 1000000 | tf_op jit(solution)/shard_map/second/pallas_call | solution.py:344
  (1 shorter events, 0.0 us)
Async XLA Ops:
  1.6 10.0 %collective-permute-start = (f32[4,160,128]{2,1,0:T(8,128)S(1)}, f32[4,160,128]{2,1,0:T(8,128)S(1)}, u32[]{:S(2)}, u32[]{:S(2)}) collective-permute-start(f32[4,160,128]{2,1,0:T(8,128)S(1)} %get-tuple-element.49), channel_id=1, source_target_pairs={{0,1},{1,0},{2,3},{3,2},{4,5},{5,4},{6,7},{7,6},{8,9},{9,8},{10,11... | collective-permute-start | bytes 983048 | tf_op jit(solution)/shard_map/ppermute | solution.py:438
  11.6 12.5 %copy-start.2 = (bf16[256,1024]{1,0:T(8,128)(2,1)S(1)}, bf16[256,1024]{1,0:T(8,128)(2,1)}, u32[]{:S(2)}) copy-start(bf16[256,1024]{1,0:T(8,128)(2,1)} %k_ref.1) | copy-start | bytes 1572868
  11.6 16.2 %copy-start = (bf16[256,1024]{1,0:T(8,128)(2,1)S(1)}, bf16[256,1024]{1,0:T(8,128)(2,1)}, u32[]{:S(2)}) copy-start(bf16[256,1024]{1,0:T(8,128)(2,1)} %v_ref.3) | copy-start | bytes 1572868
  12.8 18.0 %all-to-all-start = ((f32[32,5,4,128]{3,2,1,0:T(4,128)}), f32[32,5,4,128]{3,2,1,0:T(4,128)S(1)}, u32[]{:S(2)}, u32[]{:S(2)}) async-start(f32[32,5,4,128]{3,2,1,0:T(4,128)} %bitcast.2), calls=%async_computation | async-start | bytes 655360 | tf_op jit(solution)/shard_map/all_to_all | solution.py:434
  20.3 3.8 %collective-permute-start.1 = (f32[4,160,128]{2,1,0:T(8,128)S(1)}, f32[4,160,128]{2,1,0:T(8,128)S(1)}, u32[]{:S(2)}, u32[]{:S(2)}) collective-permute-start(f32[4,160,128]{2,1,0:T(8,128)S(1)} %get-tuple-element.53), channel_id=1, source_target_pairs={{0,1},{1,0},{2,3},{3,2},{4,5},{5,4},{6,7},{7,6},{8,9},{9,8},{10,11... | collective-permute-start | bytes 983048 | tf_op jit(solution)/shard_map/ppermute | solution.py:438
  24.1 7.4 %copy-start.3 = (f32[4,160,128]{2,1,0:T(8,128)}, f32[4,160,128]{2,1,0:T(8,128)S(1)}, u32[]{:S(2)}) copy-start(f32[4,160,128]{2,1,0:T(8,128)S(1)} %collective-permute-done.1.low_ref) | copy-start | bytes 983044
  24.1 30.2 %collective-permute-start.2 = (bf16[256,1024]{1,0:T(8,128)(2,1)S(1)}, bf16[256,1024]{1,0:T(8,128)(2,1)S(1)}, u32[]{:S(2)}, u32[]{:S(2)}) collective-permute-start(bf16[256,1024]{1,0:T(8,128)(2,1)S(1)} %copy-done.2), channel_id=1, source_target_pairs={{0,1},{1,2},{2,3},{3,4},{4,5},{5,6},{6,7},{7,8},{8,9},{9,10},{10,1... | collective-permute-start | bytes 1572872 | tf_op jit(solution)/shard_map/ppermute | solution.py:461
  27.8 26.5 %collective-permute-start.3 = (bf16[256,1024]{1,0:T(8,128)(2,1)S(1)}, bf16[256,1024]{1,0:T(8,128)(2,1)S(1)}, u32[]{:S(2)}, u32[]{:S(2)}) collective-permute-start(bf16[256,1024]{1,0:T(8,128)(2,1)S(1)} %copy-done), channel_id=1, source_target_pairs={{0,1},{1,2},{2,3},{3,4},{4,5},{5,6},{6,7},{7,8},{8,9},{9,10},{10,1... | collective-permute-start | bytes 1572872 | tf_op jit(solution)/shard_map/ppermute | solution.py:462
  31.5 7.0 %copy-start.5 = (bf16[256,256]{1,0:T(8,128)(2,1)S(1)}, bf16[256,256]{1,0:T(8,128)(2,1)}, u32[]{:S(2)}) copy-start(bf16[256,256]{1,0:T(8,128)(2,1)} %fk_ref) | copy-start | bytes 393220
  31.5 7.0 %copy-start.6 = (bf16[256,256]{1,0:T(8,128)(2,1)S(1)}, bf16[256,256]{1,0:T(8,128)(2,1)}, u32[]{:S(2)}) copy-start(bf16[256,256]{1,0:T(8,128)(2,1)} %fq_ref) | copy-start | bytes 393220
  31.5 14.4 %all-to-all-start.1 = ((f32[8,5,4,128]{3,2,1,0:T(4,128)}), f32[8,5,4,128]{3,2,1,0:T(4,128)S(1)}, u32[]{:S(2)}, u32[]{:S(2)}) async-start(f32[8,5,4,128]{3,2,1,0:T(4,128)} %broadcast_in_dim.3), calls=%async_computation.1 | async-start | bytes 163840 | tf_op jit(solution)/shard_map/all_to_all | solution.py:434
  38.5 1.0 %copy-start.4 = (f32[4,160,128]{2,1,0:T(8,128)S(1)}, f32[4,160,128]{2,1,0:T(8,128)}, u32[]{:S(2)}) copy-start(f32[4,160,128]{2,1,0:T(8,128)} %copy-done.3) | copy-start | bytes 983044
  43.6 10.7 %copy-start.1 = (bf16[256,1024]{1,0:T(8,128)(2,1)S(1)}, bf16[256,1024]{1,0:T(8,128)(2,1)}, u32[]{:S(2)}) copy-start(bf16[256,1024]{1,0:T(8,128)(2,1)} %q_ref) | copy-start | bytes 1572868
  46.6 17.6 %all-to-all-start.2 = ((f32[32,5,4,128]{3,2,1,0:T(4,128)}), f32[32,5,4,128]{3,2,1,0:T(4,128)S(1)}, u32[]{:S(2)}, u32[]{:S(2)}) async-start(f32[32,5,4,128]{3,2,1,0:T(4,128)} %bitcast.5), calls=%async_computation.2 | async-start | bytes 655360 | tf_op jit(solution)/shard_map/all_to_all | solution.py:434
  64.2 7.7 %collective-permute-start.4 = (f32[4,160,128]{2,1,0:T(8,128)S(1)}, f32[4,160,128]{2,1,0:T(8,128)S(1)}, u32[]{:S(2)}, u32[]{:S(2)}) collective-permute-start(f32[4,160,128]{2,1,0:T(8,128)S(1)} %bitcast.10), channel_id=1, source_target_pairs={{0,1},{1,0},{2,3},{3,2},{4,5},{5,4},{6,7},{7,6},{8,9},{9,8},{10,11... | collective-permute-start | bytes 983048 | tf_op jit(solution)/shard_map/ppermute | solution.py:438

commit v5 on v4

--- a/solution.py
+++ b/solution.py
@@ -99,23 +99,15 @@
         chip_ref[i] = state + got_ref[i]
 
 
-def inner_kernel(p_ref, out_ref):
+def spread_kernel(y_ref, p_ref, py_ref, out_ref):
+    y = y_ref[0]
     run = jnp.zeros((PROWS, LANES), F32)
+    for k in range(8):
+        run = run + jnp.where(k < y, py_ref[PROWS * k : PROWS * (k + 1)], F32(0.0))
     for k in range(PIECES):
         at = slice(PROWS * k, PROWS * (k + 1))
         out_ref[at] = run
         run = run + p_ref[at]
-
-
-def spread_kernel(y_ref, inner_ref, py_ref, out_ref):
-    y = y_ref[0]
-    outer = jnp.zeros((PROWS, LANES), F32)
-    for k in range(8):
-        outer = outer + jnp.where(k < y, py_ref[PROWS * k : PROWS * (k + 1)], F32(0.0))
-    twice = jnp.concatenate([outer, outer], 0)
-    for k in range(PIECES // 2):
-        at = slice(2 * PROWS * k, 2 * PROWS * (k + 1))
-        out_ref[at] = inner_ref[at] + twice
 
 
 def split3(x):
@@ -377,14 +369,10 @@
     )(core, kt, v, got)
 
 
-def inner(pieces):
+def spread(y, pieces, rows):
     flat = shape(PIECES * PROWS, LANES)
-    return call(inner_kernel, [VM], [(flat, VM)], [], 2 * 10**9, 10**6, "inner")(pieces.reshape(flat.shape))[0]
-
-
-def spread(y, before, rows):
-    return call(spread_kernel, [SM, VM, VM], [(shape(PIECES * PROWS, LANES), VM)], [], 10**6, 10**6, "spread")(
-        y, before, rows.reshape(-1, LANES)
+    return call(spread_kernel, [SM, VM, VM], [(flat, VM)], [], 10**6, 10**6, "spread")(
+        y, pieces.reshape(flat.shape), rows.reshape(-1, LANES)
     )[0]
 
 
@@ -464,10 +452,9 @@
     total = jnp.broadcast_to(jnp.sum(pieces, 0), (8, *PIECE))
     total, pieces, low, fq, fk = after(total, pieces, low, fq, fk)
     rows = exchange(total, "y")
-    before = inner(pieces)
     qf, num, den = intra(core, fq, fk, v, low, got)
-    rows, before, qf, num, den = after(rows, before, qf, num, den)
-    back = spread(scalar(lax.axis_index("y")), before, rows)
+    rows, qf, num, den = after(rows, qf, num, den)
+    back = spread(scalar(lax.axis_index("y")), pieces, rows)
     back, wq = after(back.reshape(PIECES, *PIECE), wq)
     mine = exchange(back, ("x", "z"))
     win = window(start, wq, wk, v, hk, hv)

time: 74.2 us -> 74 us (level)
  waiting for transfers between devices: 9.71 us -> 10.7 us
  local copies, waits for them, and re-layouts: 1.64 us -> 0.67 us
    unnamed x14 -> x10, local copies, waits for them, and re-layouts: 0.99 us -> 0.02 us
    all_to_all x3, waiting for transfers between devices: 7.07 us -> 8.02 us  [exchange(): return lax.all_to_all(array, axes, split_axis=0, concat_axis=0, tiled=True)]
    pallas_call x9 -> x8, Pallas kernels: 16.4 us -> 16.4 us  [call(): made(*(pltpu.with_memory_space_constraint(a, k) if k == HB else a for a,...]
where the time goes in v5:
time: 74 us; the launch traced here: 73.5 us
  starting transfers between devices  45.5 us (61%)
  Pallas kernels  16.4 us (22%)
  waiting for transfers between devices  10.7 us (14%)
    all_to_all x3, starting transfers between devices, exchange(): return lax.all_to_all(array, axes, split_axis=0, concat_axis=0, tiled=True)  22 us
    ppermute x3, starting transfers between devices, swap(): return lax.ppermute(array, 'c', [(0, 1), (1, 0)])  17.8 us
    pallas_call x8, Pallas kernels, call(): made(*(pltpu.with_memory_space_constraint(a, k) if k == HB else a for a,...  16.4 us
    all_to_all x3, waiting for transfers between devices, exchange(): return lax.all_to_all(array, axes, split_axis=0, concat_axis=0, tiled=True)  8.02 us
    ppermute x1, starting transfers between devices, body(): hk = lax.ppermute(wk_out, AXES, pairs)  3.67 us
    ppermute x3, waiting for transfers between devices, swap(): return lax.ppermute(array, 'c', [(0, 1), (1, 0)])  2.63 us
    ppermute x1, starting transfers between devices, body(): hv = lax.ppermute(v_out, AXES, pairs)  2.04 us
  transfers between devices with their start and end apart: 8, of which 6 were waited for; matrix products, arithmetic and copies ran while one was open for 1% of the time, Pallas kernels for 16%

profile of v5, /device:TPU:1, one launch (start us, length us, event | category | flops | bytes accessed | tf_op | source)
XLA Modules:
  0.0 73.5 jit_solution(3814453100755668382)
XLA Ops:
  0.0 1.6 %other.1 = (f32[4,160,128]{2,1,0:T(8,128)S(1)}, f32[256,256]{1,0:T(8,128)S(1)}, bf16[256,1024]{1,0:T(8,128)(2,1)S(1)}) custom-call(s32[1]{0:T(128)} %bitcast.core_ref, bf16[256,256]{1,0:T(8,128)(2,1)} %fk_ref, bf16[256,1024]{1,0:T(8,128)(2,1)} %v_ref.3), custom_call_target="tpu_custom_call" | custom-call | flops 1000000000 | bytes 5000000 | tf_op jit(solution)/shard_map/other/pallas_call | solution.py:336
  1.6 8.8 %collective-permute-start = (f32[4,160,128]{2,1,0:T(8,128)S(1)}, f32[4,160,128]{2,1,0:T(8,128)S(1)}, u32[]{:S(2)}, u32[]{:S(2)}) collective-permute-start(f32[4,160,128]{2,1,0:T(8,128)S(1)} %get-tuple-element.48), channel_id=1, source_target_pairs={{0,1},{1,0},{2,3},{3,2},{4,5},{5,4},{6,7},{7,6},{8,9},{9,8},{10,11... | collective-permute-start | bytes 983048 | tf_op jit(solution)/shard_map/ppermute | solution.py:426
  10.4 1.2 %collective-permute-done.got_ref.high_ref = f32[4,160,128]{2,1,0:T(8,128)S(1)} collective-permute-done((f32[4,160,128]{2,1,0:T(8,128)S(1)}, f32[4,160,128]{2,1,0:T(8,128)S(1)}, u32[]{:S(2)}, u32[]{:S(2)}) %collective-permute-start) | collective-permute-done | bytes 327712 | tf_op jit(solution)/shard_map/ppermute | solution.py:426
  11.6 0.0 copy-start.2
  11.6 0.0 copy-start
  11.6 0.0 copy-start.3
  11.6 0.0 copy-start.4
  11.6 1.2 %chip.1 = (f32[4,160,128]{2,1,0:T(8,128)S(1)}, f32[4,160,128]{2,1,0:T(8,128)}) custom-call(s32[1]{0:T(128)} %bitcast.core_ref, f32[256,256]{1,0:T(8,128)S(1)} %get-tuple-element.46.kt_ref, bf16[256,1024]{1,0:T(8,128)(2,1)S(1)} %get-tuple-element.47.v_ref, f32[4,160,128]{2,1,0:T(8,128)S(1)} %collective-permute-done.got_ref.high_ref), custom_call_target="tpu_custom_call" | custom-call | flops 1000000000 | bytes 1000000 | tf_op jit(solution)/shard_map/chip/pallas_call | solution.py:336
  12.8 7.5 %all-to-all-start = ((f32[32,5,4,128]{3,2,1,0:T(4,128)}), f32[32,5,4,128]{3,2,1,0:T(4,128)S(1)}, u32[]{:S(2)}, u32[]{:S(2)}) async-start(f32[32,5,4,128]{3,2,1,0:T(4,128)} %bitcast.2), calls=%async_computation | async-start | bytes 655360 | tf_op jit(solution)/shard_map/all_to_all | solution.py:422
  20.3 2.6 %collective-permute-start.1 = (f32[4,160,128]{2,1,0:T(8,128)S(1)}, f32[4,160,128]{2,1,0:T(8,128)S(1)}, u32[]{:S(2)}, u32[]{:S(2)}) collective-permute-start(f32[4,160,128]{2,1,0:T(8,128)S(1)} %get-tuple-element.52), channel_id=1, source_target_pairs={{0,1},{1,0},{2,3},{3,2},{4,5},{5,4},{6,7},{7,6},{8,9},{9,8},{10,11... | collective-permute-start | bytes 983048 | tf_op jit(solution)/shard_map/ppermute | solution.py:426
  22.9 1.2 %collective-permute-done.1.low_ref = f32[4,160,128]{2,1,0:T(8,128)S(1)} collective-permute-done((f32[4,160,128]{2,1,0:T(8,128)S(1)}, f32[4,160,128]{2,1,0:T(8,128)S(1)}, u32[]{:S(2)}, u32[]{:S(2)}) %collective-permute-start.1) | collective-permute-done | bytes 327712 | tf_op jit(solution)/shard_map/ppermute | solution.py:426
  24.1 0.0 copy-done.2
  24.1 3.7 %collective-permute-start.2 = (bf16[256,1024]{1,0:T(8,128)(2,1)S(1)}, bf16[256,1024]{1,0:T(8,128)(2,1)S(1)}, u32[]{:S(2)}, u32[]{:S(2)}) collective-permute-start(bf16[256,1024]{1,0:T(8,128)(2,1)S(1)} %copy-done.2), channel_id=1, source_target_pairs={{0,1},{1,2},{2,3},{3,4},{4,5},{5,6},{6,7},{7,8},{8,9},{9,10},{10,1... | collective-permute-start | bytes 1572872 | tf_op jit(solution)/shard_map/ppermute | solution.py:449
  27.8 0.0 copy-done
  27.8 2.0 %collective-permute-start.3 = (bf16[256,1024]{1,0:T(8,128)(2,1)S(1)}, bf16[256,1024]{1,0:T(8,128)(2,1)S(1)}, u32[]{:S(2)}, u32[]{:S(2)}) collective-permute-start(bf16[256,1024]{1,0:T(8,128)(2,1)S(1)} %copy-done), channel_id=1, source_target_pairs={{0,1},{1,2},{2,3},{3,4},{4,5},{5,6},{6,7},{7,8},{8,9},{9,10},{10,1... | collective-permute-start | bytes 1572872 | tf_op jit(solution)/shard_map/ppermute | solution.py:450
  29.8 0.9 %all-to-all-done = f32[32,5,4,128]{3,2,1,0:T(4,128)S(1)} async-done(((f32[32,5,4,128]{3,2,1,0:T(4,128)}), f32[32,5,4,128]{3,2,1,0:T(4,128)S(1)}, u32[]{:S(2)}, u32[]{:S(2)}) %all-to-all-start) | async-done | bytes 327712 | tf_op jit(solution)/shard_map/all_to_all | solution.py:422
  30.7 0.1 reduce_sum.9
  30.8 0.6 broadcast_in_dim.3
  31.5 6.8 %all-to-all-start.1 = ((f32[8,5,4,128]{3,2,1,0:T(4,128)}), f32[8,5,4,128]{3,2,1,0:T(4,128)S(1)}, u32[]{:S(2)}, u32[]{:S(2)}) async-start(f32[8,5,4,128]{3,2,1,0:T(4,128)} %broadcast_in_dim.3), calls=%async_computation.1 | async-start | bytes 163840 | tf_op jit(solution)/shard_map/all_to_all | solution.py:422
  38.3 0.0 copy-done.3
  38.3 0.0 copy-done.4
  38.3 4.1 %intra.1 = (bf16[20,256,128]{2,1,0:T(8,128)(2,1)}, f32[4,256,256]{2,1,0:T(8,128)}, f32[256,128]{1,0:T(8,128)}) custom-call(s32[1]{0:T(128)} %bitcast.core_ref, bf16[256,256]{1,0:T(8,128)(2,1)S(1)} %copy-done.4, bf16[256,256]{1,0:T(8,128)(2,1)S(1)} %copy-done.3, bf16[256,1024]{1,0:T(8,128)(2,1)S(1)} %copy-done, ...), custom_call_target="tpu_custom_call" | custom-call | flops 2000000000 | bytes 16000000 | tf_op jit(solution)/shard_map/intra/pallas_call | solution.py:336
  42.4 0.0 copy-start.1
  42.4 3.3 %all-to-all-done.1 = f32[8,5,4,128]{3,2,1,0:T(4,128)S(1)} async-done(((f32[8,5,4,128]{3,2,1,0:T(4,128)}), f32[8,5,4,128]{3,2,1,0:T(4,128)S(1)}, u32[]{:S(2)}, u32[]{:S(2)}) %all-to-all-start.1) | async-done | bytes 81952 | tf_op jit(solution)/shard_map/all_to_all | solution.py:422
  45.7 0.8 %spread.1 = f32[640,128]{1,0:T(8,128)} custom-call(s32[1]{0:T(128)} %bitcast.1.y_ref, f32[640,128]{1,0:T(8,128)S(1)} %bitcast.8, f32[160,128]{1,0:T(8,128)S(1)} %bitcast.9), custom_call_target="tpu_custom_call" | custom-call | flops 1000000 | bytes 1000000 | tf_op jit(solution)/shard_map/spread/pallas_call | solution.py:336
  46.5 7.6 %all-to-all-start.2 = ((f32[32,5,4,128]{3,2,1,0:T(4,128)}), f32[32,5,4,128]{3,2,1,0:T(4,128)S(1)}, u32[]{:S(2)}, u32[]{:S(2)}) async-start(f32[32,5,4,128]{3,2,1,0:T(4,128)} %bitcast.5), calls=%async_computation.2 | async-start | bytes 655360 | tf_op jit(solution)/shard_map/all_to_all | solution.py:422
  54.1 0.0 collective-permute-done.2.hk_ref
  54.1 0.0 collective-permute-done.3.hv_ref
  54.1 0.0 copy-done.1
  54.2 4.1 %window.1.win_hbm = f32[4,256,256]{2,1,0:T(8,128)} custom-call(s32[1]{0:T(128)} %bitcast.6.start_ref, bf16[256,1024]{1,0:T(8,128)(2,1)S(1)} %copy-done.1, bf16[256,1024]{1,0:T(8,128)(2,1)S(1)} %copy-done.2, bf16[256,1024]{1,0:T(8,128)(2,1)S(1)} %copy-done, bf16[256,1024]{1,0:T(8,128)(2,1)S(1)} %collective-permute-done.2.hk_ref, ...), custom_call_target="tpu_custom_call" | custom-call | flops 2000000000 | bytes 16000000 | tf_op jit(solution)/shard_map/window/pallas_call | solution.py:336
  58.3 1.9 %stage.1 = (bf16[10,256,128]{2,1,0:T(8,128)(2,1)S(1)}, f32[2,256,256]{2,1,0:T(8,128)S(1)}, f32[2,256,256]{2,1,0:T(8,128)S(1)}, bf16[10,256,128]{2,1,0:T(8,128)(2...) custom-call(s32[1]{0:T(128)} %bitcast.core_ref, bf16[20,256,128]{2,1,0:T(8,128)(2,1)} %get-tuple-element.66.qf_hbm, ...), custom_call_target="tpu_custom_call" | custom-call | flops 1000000000 | bytes 10000000 | tf_op jit(solution)/shard_map/stage/pallas_call | solution.py:336
  60.2 3.9 %all-to-all-done.2 = f32[32,5,4,128]{3,2,1,0:T(4,128)S(1)} async-done(((f32[32,5,4,128]{3,2,1,0:T(4,128)}), f32[32,5,4,128]{3,2,1,0:T(4,128)S(1)}, u32[]{:S(2)}, u32[]{:S(2)}) %all-to-all-start.2) | async-done | bytes 327712 | tf_op jit(solution)/shard_map/all_to_all | solution.py:422
  64.0 6.5 %collective-permute-start.4 = (f32[4,160,128]{2,1,0:T(8,128)S(1)}, f32[4,160,128]{2,1,0:T(8,128)S(1)}, u32[]{:S(2)}, u32[]{:S(2)}) collective-permute-start(f32[4,160,128]{2,1,0:T(8,128)S(1)} %bitcast.10), channel_id=1, source_target_pairs={{0,1},{1,0},{2,3},{3,2},{4,5},{5,4},{6,7},{7,6},{8,9},{9,8},{10,11... | collective-permute-start | bytes 983048 | tf_op jit(solution)/shard_map/ppermute | solution.py:426
  70.5 1.1 %first.1 = (bf16[2,256,256]{2,1,0:T(8,128)(2,1)S(1)}, f32[2,256,256]{2,1,0:T(8,128)S(1)}) custom-call(s32[1]{0:T(128)} %bitcast.core_ref, f32[4,160,128]{2,1,0:T(8,128)S(1)} %bitcast.11, bf16[10,256,128]{2,1,0:T(8,128)(2,1)S(1)} %get-tuple-element.82.qf_ref, f32[2,256,256]{2,1,0:T(8,128)S(1)} %get-tuple-element.83.num_ref, ...), custom_call_target="tpu_custom_call" | custom-call | flops 2000000000 | bytes 1000000 | tf_op jit(solution)/shard_map/first/pallas_call | solution.py:336
  71.6 0.2 collective-permute-done.4.p_ref
  71.8 1.7 %second.1 = bf16[256,1024]{1,0:T(8,128)(2,1)} custom-call(s32[1]{0:T(128)} %bitcast.core_ref, f32[4,160,128]{2,1,0:T(8,128)S(1)} %collective-permute-done.4.p_ref, bf16[10,256,128]{2,1,0:T(8,128)(2,1)S(1)} %get-tuple-element.79.qf_ref, f32[2,256,256]{2,1,0:T(8,128)S(1)} %get-tuple-element.80.num_ref, f32[256,128]{1,0:T(8,128)S(1)} %get-tuple-element.81.den_ref, ...), custom_call_target="tpu_custom_call" | custom-call | flops 2000000000 | bytes 1000000 | tf_op jit(solution)/shard_map/second/pallas_call | solution.py:336
Async XLA Ops:
  1.6 10.0 %collective-permute-start = (f32[4,160,128]{2,1,0:T(8,128)S(1)}, f32[4,160,128]{2,1,0:T(8,128)S(1)}, u32[]{:S(2)}, u32[]{:S(2)}) collective-permute-start(f32[4,160,128]{2,1,0:T(8,128)S(1)} %get-tuple-element.48), channel_id=1, source_target_pairs={{0,1},{1,0},{2,3},{3,2},{4,5},{5,4},{6,7},{7,6},{8,9},{9,8},{10,11... | collective-permute-start | bytes 983048 | tf_op jit(solution)/shard_map/ppermute | solution.py:426
  11.6 12.5 %copy-start.2 = (bf16[256,1024]{1,0:T(8,128)(2,1)S(1)}, bf16[256,1024]{1,0:T(8,128)(2,1)}, u32[]{:S(2)}) copy-start(bf16[256,1024]{1,0:T(8,128)(2,1)} %k_ref.1) | copy-start | bytes 1572868
  11.6 16.2 %copy-start = (bf16[256,1024]{1,0:T(8,128)(2,1)S(1)}, bf16[256,1024]{1,0:T(8,128)(2,1)}, u32[]{:S(2)}) copy-start(bf16[256,1024]{1,0:T(8,128)(2,1)} %v_ref.3) | copy-start | bytes 1572868
  11.6 26.7 %copy-start.3 = (bf16[256,256]{1,0:T(8,128)(2,1)S(1)}, bf16[256,256]{1,0:T(8,128)(2,1)}, u32[]{:S(2)}) copy-start(bf16[256,256]{1,0:T(8,128)(2,1)} %fk_ref) | copy-start | bytes 393220
  11.6 26.7 %copy-start.4 = (bf16[256,256]{1,0:T(8,128)(2,1)S(1)}, bf16[256,256]{1,0:T(8,128)(2,1)}, u32[]{:S(2)}) copy-start(bf16[256,256]{1,0:T(8,128)(2,1)} %fq_ref) | copy-start | bytes 393220
  12.8 18.0 %all-to-all-start = ((f32[32,5,4,128]{3,2,1,0:T(4,128)}), f32[32,5,4,128]{3,2,1,0:T(4,128)S(1)}, u32[]{:S(2)}, u32[]{:S(2)}) async-start(f32[32,5,4,128]{3,2,1,0:T(4,128)} %bitcast.2), calls=%async_computation | async-start | bytes 655360 | tf_op jit(solution)/shard_map/all_to_all | solution.py:422
  20.3 3.8 %collective-permute-start.1 = (f32[4,160,128]{2,1,0:T(8,128)S(1)}, f32[4,160,128]{2,1,0:T(8,128)S(1)}, u32[]{:S(2)}, u32[]{:S(2)}) collective-permute-start(f32[4,160,128]{2,1,0:T(8,128)S(1)} %get-tuple-element.52), channel_id=1, source_target_pairs={{0,1},{1,0},{2,3},{3,2},{4,5},{5,4},{6,7},{7,6},{8,9},{9,8},{10,11... | collective-permute-start | bytes 983048 | tf_op jit(solution)/shard_map/ppermute | solution.py:426
  24.1 30.0 %collective-permute-start.2 = (bf16[256,1024]{1,0:T(8,128)(2,1)S(1)}, bf16[256,1024]{1,0:T(8,128)(2,1)S(1)}, u32[]{:S(2)}, u32[]{:S(2)}) collective-permute-start(bf16[256,1024]{1,0:T(8,128)(2,1)S(1)} %copy-done.2), channel_id=1, source_target_pairs={{0,1},{1,2},{2,3},{3,4},{4,5},{5,6},{6,7},{7,8},{8,9},{9,10},{10,1... | collective-permute-start | bytes 1572872 | tf_op jit(solution)/shard_map/ppermute | solution.py:449
  27.8 26.3 %collective-permute-start.3 = (bf16[256,1024]{1,0:T(8,128)(2,1)S(1)}, bf16[256,1024]{1,0:T(8,128)(2,1)S(1)}, u32[]{:S(2)}, u32[]{:S(2)}) collective-permute-start(bf16[256,1024]{1,0:T(8,128)(2,1)S(1)} %copy-done), channel_id=1, source_target_pairs={{0,1},{1,2},{2,3},{3,4},{4,5},{5,6},{6,7},{7,8},{8,9},{9,10},{10,1... | collective-permute-start | bytes 1572872 | tf_op jit(solution)/shard_map/ppermute | solution.py:450
  31.5 14.2 %all-to-all-start.1 = ((f32[8,5,4,128]{3,2,1,0:T(4,128)}), f32[8,5,4,128]{3,2,1,0:T(4,128)S(1)}, u32[]{:S(2)}, u32[]{:S(2)}) async-start(f32[8,5,4,128]{3,2,1,0:T(4,128)} %broadcast_in_dim.3), calls=%async_computation.1 | async-start | bytes 163840 | tf_op jit(solution)/shard_map/all_to_all | solution.py:422
  42.4 11.7 %copy-start.1 = (bf16[256,1024]{1,0:T(8,128)(2,1)S(1)}, bf16[256,1024]{1,0:T(8,128)(2,1)}, u32[]{:S(2)}) copy-start(bf16[256,1024]{1,0:T(8,128)(2,1)} %q_ref) | copy-start | bytes 1572868
  46.5 17.6 %all-to-all-start.2 = ((f32[32,5,4,128]{3,2,1,0:T(4,128)}), f32[32,5,4,128]{3,2,1,0:T(4,128)S(1)}, u32[]{:S(2)}, u32[]{:S(2)}) async-start(f32[32,5,4,128]{3,2,1,0:T(4,128)} %bitcast.5), calls=%async_computation.2 | async-start | bytes 655360 | tf_op jit(solution)/shard_map/all_to_all | solution.py:422
  64.0 7.7 %collective-permute-start.4 = (f32[4,160,128]{2,1,0:T(8,128)S(1)}, f32[4,160,128]{2,1,0:T(8,128)S(1)}, u32[]{:S(2)}, u32[]{:S(2)}) collective-permute-start(f32[4,160,128]{2,1,0:T(8,128)S(1)} %bitcast.10), channel_id=1, source_target_pairs={{0,1},{1,0},{2,3},{3,2},{4,5},{5,4},{6,7},{7,6},{8,9},{9,8},{10,11... | collective-permute-start | bytes 983048 | tf_op jit(solution)/shard_map/ppermute | solution.py:426
